TPU v7x, 32 devices: a whole 2x2x4 slice. The times are simulated.
32 devices in a mesh: station: 2 (over x), tm: 16 (over z, y, core).
Axes of the slice: x: 2, y: 2, z: 4, core: 2. Of those that a mesh axis runs over, the one named last changes fastest.
Arguments:
- features: bfloat16 [524288, 256], P(('station', 'tm')), may hold values from -8 to 8
- targets: bfloat16 [524288], P(('station', 'tm')), may hold values from -6 to 6
- station_ids: int32 [524288], P(('station', 'tm')), may hold values from 0 to 127
- lead_heads: int32 [524288], P(('station', 'tm')), may hold values from 0 to 15, as said below
- station_weight: float32 [2, 128], P('station'), may hold values from 0.2 to 5
Outputs:
- leverage: float32 [524288], P(('station', 'tm'))
- zscores: float32 [16, 256], replicated
- inverse_factor: float32 [16, 256, 256], P(None, 'tm')
Inputs may be any that keep to these rules, and one draw needn't show every extreme that they name: lead_heads is constant over each aligned block of 1024 rows.
All inputs are finite; a program needn't handle non-finite values.
Results may differ from a plain program's by a relative error of at most 0.008.
Values sent between devices are 32-bit elements; how exact they have to be, the bound alone decides.
A program may use at most 128 MiB of HBM per device.

v0:
```python
import math

import jax
import jax.numpy as jnp
from jax import lax
from jax.sharding import PartitionSpec as P

HEADS = 16
BLK = 1024


def factor_heads(gram_sum, moment):
    feat_width = gram_sum.shape[-1]
    identity = jnp.eye(feat_width, dtype=jnp.float32)
    lower_factor = jnp.linalg.cholesky(gram_sum + identity)
    inverse = lax.linalg.triangular_solve(
        lower_factor, jnp.broadcast_to(identity, gram_sum.shape), left_side=True, lower=True
    )
    inner_term = jnp.einsum("hkj,hj->hk", inverse, moment, precision=lax.Precision.HIGHEST)
    coefficient = jnp.einsum("hkj,hk->hj", inverse, inner_term, precision=lax.Precision.HIGHEST)
    spreads = jnp.sqrt(jnp.sum(inverse * inverse, axis=1))
    return (inverse, coefficient / spreads)


def local(features, targets, station_ids, lead_heads, station_weight):
    row_count, feat_width = features.shape
    station_count = station_weight.shape[1]
    block_count = row_count // BLK
    total_rows = row_count * lax.axis_size("station") * lax.axis_size("tm")
    station_pick = (
        station_ids[:, None] == jnp.arange(station_count, dtype=jnp.int32)[None, :]
    ).astype(jnp.float32)
    row_weight = jnp.dot(station_pick, station_weight[0], precision=lax.Precision.HIGHEST)
    weighted = (row_weight[:, None] * features).astype(jnp.bfloat16)
    feat_blocks = features.reshape(block_count, BLK, feat_width)
    weight_blocks = weighted.reshape(block_count, BLK, feat_width)
    target_blocks = targets.reshape(block_count, BLK)
    block_heads = lead_heads.reshape(block_count, BLK)[:, 0]
    block_pick = (block_heads[:, None] == jnp.arange(HEADS, dtype=jnp.int32)[None, :]).astype(
        jnp.float32
    )
    block_gram = jnp.einsum(
        "bri,brj->bij", weight_blocks, feat_blocks, preferred_element_type=jnp.float32
    )
    block_moment = jnp.einsum(
        "bri,br->bi", weight_blocks, target_blocks, preferred_element_type=jnp.float32
    )
    gram_sum = jnp.einsum("bh,bij->hij", block_pick, block_gram, precision=lax.Precision.HIGHEST)
    moment = jnp.einsum("bh,bi->hi", block_pick, block_moment, precision=lax.Precision.HIGHEST)
    share_gram, share_moment = (
        lax.psum_scatter(gram_sum, "station", scatter_dimension=0, tiled=True),
        lax.psum_scatter(moment, "station", scatter_dimension=0, tiled=True),
    )
    share_gram, share_moment = lax.psum((share_gram, share_moment), "tm")
    share_inverse, share_scores = factor_heads(share_gram, share_moment)
    inverse, zscores = (
        lax.all_gather(share_inverse, "station", axis=0, tiled=True),
        lax.all_gather(share_scores, "station", axis=0, tiled=True),
    )
    inverse_low = inverse.astype(jnp.bfloat16)
    picked = jnp.einsum(
        "bh,hkj->bkj",
        block_pick.astype(jnp.bfloat16),
        inverse_low,
        preferred_element_type=jnp.float32,
    ).astype(jnp.bfloat16)
    projected = jnp.einsum("bri,bki->brk", feat_blocks, picked, preferred_element_type=jnp.float32)
    sum_squares = jnp.sum(projected * projected, axis=2).reshape(row_count)
    leverage = row_weight * sum_squares * (total_rows / (HEADS * feat_width))
    piece_rows = feat_width // lax.axis_size("tm")
    own_piece = lax.dynamic_slice_in_dim(inverse, lax.axis_index("tm") * piece_rows, piece_rows, 1)
    inverse_factor = own_piece * math.sqrt(total_rows / HEADS)
    return (leverage, zscores, inverse_factor)


def solution(mesh):
    return jax.shard_map(
        local,
        mesh=mesh,
        in_specs=(
            P(("station", "tm"), None),
            P(("station", "tm")),
            P(("station", "tm")),
            P(("station", "tm")),
            P("station", None),
        ),
        out_specs=(P(("station", "tm")), P(), P(None, "tm", None)),
        check_vma=False,
    )
```

profile of v0, /device:TPU:0, one launch (start us, length us, event | category | flops | bytes accessed | tf_op | source)
XLA Modules:
  0.0 732.7 jit_solution(4970667285525582635)
XLA Ops:
  8.2 6.5 fusion
  14.7 7.9 %multiply_convert_fusion = bf16[16384,256]{1,0:T(8,128)(2,1)} fusion(bf16[16384,256]{1,0:T(8,128)(2,1)} %param.5, f32[16384]{0:T(1024)S(1)} %bitcast.70), kind=kLoop, calls=%fused_computation.3 | loop fusion | flops 12582912 | bytes 16842752 | tf_op jit(solution)/shard_map/convert_element_type | solution.py:34
  22.6 8.2 %fusion.33 = f32[16,256,256]{2,1,0:T(8,128)S(1)} fusion(bf16[16,1024,256]{2,1,0:T(8,128)(2,1)} %bitcast.66, bf16[16,1024,256]{2,1,0:T(8,128)(2,1)} %bitcast.68), kind=kOutput, calls=%fused_computation.65 | convolution fusion | flops 2147483648 | bytes 20971520 | tf_op jit(solution)/shard_map/bri,brj->bij/dot_general | solution.py:42
  30.9 5.2 fusion.1
  36.1 5.2 copy.57
  41.4 57.1 %reduce-scatter.3.cloned.1.call-done = f32[8,256,256]{1,2,0:T(8,128)} async-done(((f32[16,256,256]{1,2,0:T(8,128)}), f32[8,256,256]{1,2,0:T(8,128)}) %reduce-scatter.3.cloned.1.call-update) | async-done | bytes 2097168 | tf_op jit(solution)/shard_map/reduce_scatter | solution.py:51
  98.6 4.6 fusion.34
  105.1 95.3 %all-reduce.3.cloned.1.call-done = f32[8,256,256]{1,2,0:T(8,128)} async-done(((f32[8,256,256]{1,2,0:T(8,128)}), f32[8,256,256]{1,2,0:T(8,128)}) %all-reduce.3.cloned.1.call-update) | async-done | bytes 2097168 | tf_op jit(solution)/shard_map/psum | solution.py:54
  200.4 3.1 broadcast_add_fusion
  203.5 3.1 copy.58
  206.6 2.0 fusion.5
  210.0 93.8 %custom-call.16 = f32[8,128,128]{2,1,0:T(8,128)S(1)} custom-call(f32[8,128,128]{2,1,0:T(8,128)S(1)} %cholesky.122), custom_call_target="Cholesky" | custom-call | tf_op jit(solution)/shard_map/jit(cholesky)/cholesky | solution.py:15
  303.8 78.6 %custom-call.17 = f32[8,1,128,128]{2,3,1,0:T(8,128)S(1)} custom-call(f32[8,1,128,128]{3,2,1,0:T(8,128)S(1)} %select_bitcast_fusion), custom_call_target="InvertDiagBlocksLowerTriangular" | custom-call | tf_op jit(solution)/shard_map/jit(cholesky)/cholesky | solution.py:15
  386.7 94.8 %custom-call.18 = f32[8,128,128]{2,1,0:T(8,128)S(1)} custom-call(f32[8,128,128]{2,1,0:T(8,128)} %convolution_subtract_fusion.1), custom_call_target="Cholesky" | custom-call | tf_op jit(solution)/shard_map/jit(cholesky)/cholesky | solution.py:15
  485.6 5.9 while.1
  486.2 2.3 bitcast_dynamic-update-slice_fusion.2
  489.2 2.3 bitcast_dynamic-update-slice_fusion.2
  491.5 158.7 %custom-call.19 = f32[8,2,128,128]{2,3,1,0:T(8,128)} custom-call(f32[8,2,128,128]{3,2,1,0:T(8,128)} %bitcast.76), custom_call_target="InvertDiagBlocksLowerTriangular" | custom-call | tf_op jit(solution)/shard_map/triangular_solve | solution.py:16
  650.2 2.2 fusion.10
  656.2 31.0 %psum.15 = f32[8,256]{1,0:T(8,128)S(1)} all-reduce(f32[8,256]{1,0:T(8,128)} %reduce-scatter.5.cloned.1.call-done), channel_id=1, replica_groups=mesh['station'=2,'tm'=16] {'tm'}, use_global_device_ids=true, to_apply=%region_8.9 | all-reduce | flops 2048 | bytes 16384 | tf_op jit(solution)/shard_map/psum | solution.py:54
  690.3 4.8 all_gather.7
  695.0 17.4 %all-gather.2.cloned.1.call-done = f32[16,256,256]{2,1,0:T(8,128)} async-done(((f32[8,256,256]{2,1,0:T(8,128)}), f32[16,256,256]{2,1,0:T(8,128)}) %all-gather.2.cloned.1.call-update) | async-done | bytes 4194320 | tf_op jit(solution)/shard_map/all_gather | solution.py:57
  712.5 4.6 fusion.7
  717.1 6.1 multiply_reduce_fusion
  (61 shorter events, 23.8 us)
Async XLA Ops:
  7.2 1.0 copy-start
  7.2 91.3 %reduce-scatter.3.cloned.1.call-start = ((), (), s32[]{:S(2)}) async-start(), calls=%async_computation.2 | async-start | bytes 6291456 | tf_op jit(solution)/shard_map/reduce_scatter | solution.py:51
  41.4 57.2 %copy-start.6 = (bf16[16384]{0:T(1024)(128)(2,1)S(1)}, bf16[16384]{0:T(1024)(128)(2,1)}, u32[]{:S(2)}) copy-start(bf16[16384]{0:T(1024)(128)(2,1)} %param.6) | copy-start | bytes 98308
  41.4 159.0 %all-reduce.3.cloned.1.call-start = ((), (), s32[]{:S(2)}) async-start(), calls=%async_computation.3 | async-start | bytes 4194304 | tf_op jit(solution)/shard_map/psum | solution.py:54
  98.5 557.6 %reduce-scatter.5.cloned.1.call-start = ((), (), s32[]{:S(2)}) async-start(), calls=%async_computation.5 | async-start | bytes 24576 | tf_op jit(solution)/shard_map/reduce_scatter | solution.py:52
  104.1 608.4 %all-gather.2.cloned.1.call-start = ((), (), s32[]{:S(2)}) async-start(), calls=%async_computation.4 | async-start | bytes 6291456 | tf_op jit(solution)/shard_map/all_gather | solution.py:57
  203.5 3.1 copy-start.1
  208.6 1.4 copy-start.3
  382.4 1.6 copy-start.4
  482.3 1.4 copy-start.2
  650.2 3.2 copy-start.5
Sparse Core Ops, SparseCore 0:
  41.5 56.9 reduce-scatter.2
  102.5 97.8 all-reduce.2
  203.1 9.0 reduce-scatter.4
  656.2 56.1 all-gather.1
where the time goes:
time: 734 us; the launch traced here: 733 us
  other arithmetic  446 us (61%)
  waiting for transfers between devices  170 us (23%)
  matrix products  46.1 us (6%)
  blocking collectives  35.8 us (5%)
  local copies, waits for them, and re-layouts  20.3 us (3%)
  between operations  14 us (2%)
    another operation x9, other arithmetic, factor_heads(): lower_factor = jnp.linalg.cholesky(gram_sum + identity)  269 us
    another operation x4, other arithmetic, factor_heads(): lax.linalg.triangular_solve(lower_factor, jnp.broadcast_to(identity, gram...  161 us
    psum x1, waiting for transfers between devices, local(): share_gram, share_moment = lax.psum((share_gram, share_moment), 'tm')  95.3 us
    reduce_scatter x1, waiting for transfers between devices, local(): lax.psum_scatter(gram_sum, 'station', scatter_dimension=0, tiled=True)  57.1 us
    psum x1, blocking collectives, local(): share_gram, share_moment = lax.psum((share_gram, share_moment), 'tm')  31 us
    all_gather x1, waiting for transfers between devices, local(): lax.all_gather(share_inverse, 'station', axis=0, tiled=True)  17.4 us
  transfers between devices with their start and end apart: 4, of which 3 were waited for; matrix products, arithmetic and copies ran while one was open for 63% of the time, Pallas kernels for 0%

commit v1 on v0

v1 whole, which is shorter than its diff:
```python
import functools
import math

import jax
import jax.numpy as jnp
from jax import lax
from jax.experimental import pallas as pl
from jax.experimental.pallas import tpu as pltpu
from jax.sharding import PartitionSpec as P

HEADS = 16
BLK = 1024
LANES = 128
SUB = BLK // LANES
HEAD_BITS = 4
F32 = jnp.float32
HIGHEST = lax.Precision.HIGHEST
MESH = pl.DeviceIdType.MESH
PACK_ROWS = 416
VEC_ROW = 384


def bits_of(mesh_shape):
    station, tm = mesh_shape["station"], mesh_shape["tm"]
    core = ("tm", 1)
    owner = [("station", 1), ("tm", 2), ("tm", 4), ("tm", 8)]
    rest = [("station", s) for s in (2**i for i in range(1, 16)) if s < station]
    rest += [("tm", s) for s in (2**i for i in range(4, 16)) if s < tm]
    return core, owner, rest


def bit_value(bit):
    return lax.rem(lax.div(lax.axis_index(bit[0]), bit[1]), 2)


def partner(bit):
    axis, step = bit
    return {axis: lax.axis_index(axis) + (1 - 2 * bit_value(bit)) * step}


def greet(bits):
    barrier = pltpu.get_barrier_semaphore()
    for bit in bits:
        pl.semaphore_signal(barrier, inc=1, device_id=partner(bit), device_id_type=MESH)
    pl.semaphore_wait(barrier, len(bits))


def gram_kernel(heads_ref, feat_ref, ids_ref, tgt_ref, table_ref, out_ref, w_ref, acc, vec, tgt):
    step = pl.program_id(0)

    @pl.when(step == 0)
    def _():
        acc[...] = jnp.zeros_like(acc)
        vec[...] = jnp.zeros_like(vec)
        tgt[...] = tgt_ref[...].astype(F32)

    table = jnp.broadcast_to(table_ref[...], (SUB, LANES))
    weights = jnp.take_along_axis(table, ids_ref[...], axis=1, mode="promise_in_bounds")
    w_ref[...] = weights
    feat = feat_ref[...]
    turned = feat.T
    scaled = jnp.concatenate(
        [
            (turned[:, c * LANES : (c + 1) * LANES].astype(F32) * weights[c : c + 1, :]).astype(
                jnp.bfloat16
            )
            for c in range(SUB)
        ],
        axis=1,
    )
    head = heads_ref[0, 0]
    acc[head] += jnp.dot(scaled, feat, preferred_element_type=F32)
    here = tgt[pl.ds(pl.multiple_of(step * SUB, SUB), SUB), :]
    row = lax.broadcasted_iota(jnp.int32, (SUB, LANES), 0)
    spread = jnp.concatenate([jnp.where(row == c, here, 0.0) for c in range(SUB)], axis=1)
    vec[head] += lax.dot_general(
        spread.astype(jnp.bfloat16), scaled, (((1,), (1,)), ((), ())), preferred_element_type=F32
    )

    @pl.when(step == pl.num_programs(0) - 1)
    def _():
        @pl.loop(0, HEADS)
        def _(h):
            out_ref[h, 0:128, :] = acc[h, 0:128, 0:128]
            out_ref[h, 128:256, :] = 0.5 * (acc[h, 128:256, 0:128] + acc[h, 0:128, 128:256].T)
            out_ref[h, 256:384, :] = acc[h, 128:256, 128:256]
            total = jnp.sum(vec[h], axis=0, keepdims=True)
            out_ref[h, VEC_ROW:PACK_ROWS, :] = jnp.zeros((PACK_ROWS - VEC_ROW, LANES), F32)
            out_ref[h, VEC_ROW : VEC_ROW + 1, :] = total[:, 0:128]
            out_ref[h, VEC_ROW + 1 : VEC_ROW + 2, :] = total[:, 128:256]


def reduce_kernel(plan, g_ref, out_ref, acc, first, fin, *rest):
    core_bit, orders, all_bits = plan
    stage_count = len(orders[0])
    bufs = [rest[c * stage_count : (c + 1) * stage_count] for c in range(2)]
    send, recv = rest[-2:]
    half = PACK_ROWS // 2
    quarter = half // 2
    core = bit_value(core_bit)
    mine = [pl.ds(pl.multiple_of(core * half + c * quarter, 8), quarter) for c in range(2)]
    theirs = [pl.ds(pl.multiple_of((1 - core) * half + c * quarter, 8), quarter) for c in range(2)]
    greet(all_bits)
    sent = []

    def push(src, dst, chain, stage, bit):
        copy = pltpu.make_async_remote_copy(
            src_ref=src,
            dst_ref=dst,
            send_sem=send.at[chain, stage],
            recv_sem=recv.at[chain, stage],
            device_id=partner(bit),
            device_id_type=MESH,
        )
        copy.start()
        sent.append(copy)
        return copy

    flying = [
        push(g_ref.at[:, :, :, :, theirs[c]], first.at[c], c, 0, core_bit) for c in range(2)
    ]
    every = slice(None)
    index = [[every] * HEAD_BITS for _ in range(2)]
    for stage in range(stage_count + 1):
        for c in range(2):
            flying[c].wait_recv()
            if stage == 0:
                acc[c] = g_ref[:, :, :, :, mine[c], :] + first[c]
            else:
                place = (c, *index[c])
                acc[place] = acc[place] + bufs[c][stage - 1][...]
            if stage < stage_count:
                bit, dim = orders[c][stage]
                away = list(index[c])
                if dim is not None:
                    away[dim] = 1 - bit_value(bit)
                    index[c][dim] = bit_value(bit)
                flying[c] = push(acc.at[(c, *away)], bufs[c][stage], c, stage + 1, bit)
            else:
                flying[c] = push(acc.at[(c, *index[c])], fin.at[c], c, stage + 1, core_bit)
    for c in range(2):
        flying[c].wait_recv()
        out_ref[mine[c], :] = acc[(c, *index[c])]
        out_ref[theirs[c], :] = fin[c]
    for copy in sent:
        copy.wait_send()


def gather_kernel(plan, x_ref, out_ref, send, recv, send_core, recv_core):
    core_bit, orders, all_bits = plan
    half = PACK_ROWS // 2
    quarter = half // 2
    core = bit_value(core_bit)
    mine = [pl.ds(pl.multiple_of(core * half + c * quarter, 8), quarter) for c in range(2)]
    own = [None] * HEAD_BITS
    for bit, dim in orders[0]:
        own[dim] = bit_value(bit)
    out_ref[(*own,)] = x_ref[...]
    greet(all_bits)
    sent, late = [], []

    def push(place, chain, bit, send_sem, recv_sem):
        view = out_ref.at[(*place, mine[chain])]
        copy = pltpu.make_async_remote_copy(
            src_ref=view,
            dst_ref=view,
            send_sem=send_sem,
            recv_sem=recv_sem,
            device_id=partner(bit),
            device_id_type=MESH,
        )
        copy.start()
        sent.append(copy)
        return copy

    index = [list(own) for _ in range(2)]
    flying = [None, None]
    for stage in range(HEAD_BITS + 1):
        for c in range(2):
            if stage > 0:
                flying[c].wait_recv()
                bit, dim = orders[c][stage - 1]
                news = list(index[c])
                news[dim] = 1 - bit_value(bit)
                index[c][dim] = slice(None)
            if stage < HEAD_BITS:
                bit, dim = orders[c][stage]
                flying[c] = push(index[c], c, bit, send.at[c, stage], recv.at[c, stage])
            if stage > 0:
                late.append(
                    push(
                        news, c, core_bit, send_core.at[c, stage - 1], recv_core.at[c, stage - 1]
                    )
                )
    for copy in late:
        copy.wait_recv()
    for copy in sent:
        copy.wait_send()


def mm(a, b, dims):
    return lax.dot_general(a, b, (dims, ((), ())), precision=HIGHEST, preferred_element_type=F32)


def eliminate(matrix, offset):
    groups = matrix.shape[0] // 8
    rows = [matrix[8 * g : 8 * g + 8, :] for g in range(groups)]
    below = lax.broadcasted_iota(jnp.int32, (8, LANES), 0)
    for p in range(groups):
        columns = [offset + 8 * p + k for k in range(8)]
        pivots = [None] * 8
        across = [[None] * 8 for _ in range(8)]
        lines = [None] * 8
        for g in range(p, groups):
            cols = [jnp.broadcast_to(rows[g][:, j : j + 1], (8, LANES)) for j in columns]
            for k in range(8):
                if g == p:
                    pivots[k] = 1.0 / cols[k][k : k + 1, :]
                    lines[k] = rows[p][k : k + 1, :]
                    for m in range(k + 1, 8):
                        across[k][m] = cols[m][k : k + 1, :]
                factor = cols[k] * pivots[k]
                if g == p:
                    factor = jnp.where(below > k, factor, 0.0)
                for m in range(k + 1, 8):
                    cols[m] = cols[m] - factor * across[k][m]
                rows[g] = rows[g] - factor * lines[k]
    done = jnp.concatenate(rows, axis=0)
    lane = lax.broadcasted_iota(jnp.int32, done.shape, 1)
    row = lax.broadcasted_iota(jnp.int32, done.shape, 0)
    diagonal = jnp.sum(jnp.where(lane == row + offset, done, 0.0), axis=1, keepdims=True)
    return done * (1.0 / jnp.sqrt(diagonal))


def inverse_factor_128(a):
    lane = lax.broadcasted_iota(jnp.int32, (64, LANES), 1)
    row = lax.broadcasted_iota(jnp.int32, (64, LANES), 0)
    low = lane < 64
    top, bottom = a[0:64, :], a[64:128, :]
    first = eliminate(jnp.where(low, top, (lane == row + 64).astype(F32)), 0)
    x1 = jnp.where(low, pltpu.roll(first, 64, 1), 0.0)
    upper = mm(x1[:, 0:64], top, ((1,), (0,)))
    schur = bottom - mm(upper, upper, ((0,), (0,)))[64:128, :]
    second = eliminate(jnp.where(low, (lane == row).astype(F32), schur), 64)
    x2 = jnp.where(low, second, 0.0)
    across = mm(upper, x1, ((0,), (0,)))[64:128, :]
    x21 = -mm(x2[:, 0:64], across, ((1,), (0,)))
    return jnp.concatenate([x1, x21 + pltpu.roll(x2, 64, 1)], axis=0)


def factor_kernel(g_ref, out_ref):
    size = LANES
    eye = (
        lax.broadcasted_iota(jnp.int32, (size, size), 0)
        == lax.broadcasted_iota(jnp.int32, (size, size), 1)
    ).astype(F32)
    g11 = g_ref[0:128, :]
    g21 = g_ref[128:256, :]
    g22 = g_ref[256:384, :]
    x1 = inverse_factor_128(0.5 * (g11 + g11.T) + eye)
    out_ref[0:128, :] = x1
    lower = mm(g21, x1, ((1,), (1,)))
    x2 = inverse_factor_128(0.5 * (g22 + g22.T) + eye - mm(lower, lower, ((1,), (1,))))
    out_ref[256:384, :] = x2
    x21 = -mm(x2, mm(lower, x1, ((1,), (0,))), ((1,), (0,)))
    out_ref[128:256, :] = x21
    m1 = jnp.broadcast_to(g_ref[VEC_ROW : VEC_ROW + 1, :], (8, LANES))
    m2 = jnp.broadcast_to(g_ref[VEC_ROW + 1 : VEC_ROW + 2, :], (8, LANES))
    in1 = mm(m1, x1, ((1,), (1,)))
    in2 = mm(m1, x21, ((1,), (1,))) + mm(m2, x2, ((1,), (1,)))
    co1 = mm(in1, x1, ((1,), (0,))) + mm(in2, x21, ((1,), (0,)))
    co2 = mm(in2, x2, ((1,), (0,)))
    s1 = jnp.sum(x1 * x1, axis=0, keepdims=True) + jnp.sum(x21 * x21, axis=0, keepdims=True)
    s2 = jnp.sum(x2 * x2, axis=0, keepdims=True)
    out_ref[VEC_ROW:PACK_ROWS, :] = jnp.zeros((PACK_ROWS - VEC_ROW, LANES), F32)
    out_ref[VEC_ROW : VEC_ROW + 1, :] = co1[0:1, :] / jnp.sqrt(s1)
    out_ref[VEC_ROW + 1 : VEC_ROW + 2, :] = co2[0:1, :] / jnp.sqrt(s2)


def leverage_kernel(scale, place_ref, heads_ref, feat_ref, w_ref, inv_ref, lev_ref, z_ref, piece_ref):
    step = pl.program_id(0)

    @pl.when(step == 0)
    def _():
        z_ref[:, 0:128] = inv_ref[:, VEC_ROW, :]
        z_ref[:, 128:256] = inv_ref[:, VEC_ROW + 1, :]
        count = piece_ref.shape[1]
        start = place_ref[0] * count
        root = math.sqrt(scale * 2 * LANES)
        left = inv_ref[:, pl.ds(pl.multiple_of(start, 8), count), :]
        spot = pl.multiple_of(jnp.maximum(start - 128, 0) + 256, 8)
        right = inv_ref[:, pl.ds(spot, count), :]
        piece_ref[:, :, 0:128] = left * root
        piece_ref[:, :, 128:256] = jnp.where(start >= 128, right * root, 0.0)

    head = heads_ref[0, 0]
    zero = jnp.zeros((128, 128), jnp.bfloat16)
    x1 = inv_ref[head, 0:128, :].astype(jnp.bfloat16)
    x21 = inv_ref[head, 128:256, :].astype(jnp.bfloat16)
    x2 = inv_ref[head, 256:384, :].astype(jnp.bfloat16)
    low = jnp.concatenate(
        [jnp.concatenate([x1, zero], axis=1), jnp.concatenate([x21, x2], axis=1)], axis=0
    )
    turned = lax.dot_general(
        low, feat_ref[...], (((1,), (1,)), ((), ())), preferred_element_type=F32
    )
    squares = jnp.sum(turned * turned, axis=0, keepdims=True)
    for c in range(SUB):
        lev_ref[c : c + 1, :] = w_ref[c : c + 1, :] * squares[:, c * LANES : (c + 1) * LANES] * scale


def local(mesh_shape, features, targets, station_ids, lead_heads, station_weight):
    row_count, width = features.shape
    blocks = row_count // BLK
    lines = row_count // LANES
    tm = mesh_shape["tm"]
    total_rows = row_count * mesh_shape["station"] * tm
    scale = total_rows / (HEADS * width)
    ids = station_ids.reshape(lines, LANES)
    heads = lead_heads.reshape(lines, LANES)
    goals = targets.reshape(lines, LANES)
    head_spec = pl.BlockSpec((SUB, LANES), lambda b: (b, 0), memory_space=pltpu.SMEM)
    line_spec = pl.BlockSpec((SUB, LANES), lambda b: (b, 0))
    feat_spec = pl.BlockSpec((BLK, width), lambda b: (b, 0))
    big = 48 * 1024 * 1024
    packed, weights = pl.pallas_call(
        gram_kernel,
        grid=(blocks,),
        in_specs=[
            head_spec,
            feat_spec,
            line_spec,
            pl.BlockSpec((lines, LANES), lambda b: (0, 0)),
            pl.BlockSpec((1, LANES), lambda b: (0, 0)),
        ],
        out_specs=[pl.BlockSpec((HEADS, PACK_ROWS, LANES), lambda b: (0, 0, 0)), line_spec],
        out_shape=[
            jax.ShapeDtypeStruct((HEADS, PACK_ROWS, LANES), F32),
            jax.ShapeDtypeStruct((lines, LANES), F32),
        ],
        scratch_shapes=[
            pltpu.VMEM((HEADS, width, width), F32),
            pltpu.VMEM((HEADS, 8, width), F32),
            pltpu.VMEM((lines, LANES), F32),
        ],
        compiler_params=pltpu.CompilerParams(vmem_limit_bytes=big),
        name="gram",
    )(heads, features, ids, goals, station_weight)

    core_bit, owner, rest = bits_of(mesh_shape)
    named = [(bit, dim) for dim, bit in enumerate(owner)]
    x, y, z0, z1 = named
    tail = [(bit, None) for bit in rest]
    down = ([x, y, z0, z1] + tail, [y, x, z0, z1] + tail)
    up = ([z1, z0, y, x], [z1, z0, x, y])
    dims = (2,) * HEAD_BITS
    quarter = PACK_ROWS // 4
    buffers = []
    for c in range(2):
        free = HEAD_BITS
        for bit, dim in down[c]:
            free -= dim is not None
            buffers.append(pltpu.VMEM((2,) * free + (quarter, LANES), F32))
    vmem = pl.BlockSpec(memory_space=pltpu.VMEM)
    summed = pl.pallas_call(
        functools.partial(reduce_kernel, (core_bit, down, [core_bit] + owner + rest)),
        out_shape=jax.ShapeDtypeStruct((PACK_ROWS, LANES), F32),
        in_specs=[vmem],
        out_specs=vmem,
        scratch_shapes=[
            pltpu.VMEM((2, *dims, quarter, LANES), F32),
            pltpu.VMEM((2, *dims, quarter, LANES), F32),
            pltpu.VMEM((2, quarter, LANES), F32),
            *buffers,
            pltpu.SemaphoreType.DMA((2, len(down[0]) + 2)),
            pltpu.SemaphoreType.DMA((2, len(down[0]) + 2)),
        ],
        compiler_params=pltpu.CompilerParams(
            collective_id=0, has_side_effects=True, vmem_limit_bytes=big
        ),
        name="reduce",
    )(packed.reshape(*dims, PACK_ROWS, LANES))

    solved = pl.pallas_call(
        factor_kernel,
        out_shape=jax.ShapeDtypeStruct((PACK_ROWS, LANES), F32),
        in_specs=[vmem],
        out_specs=vmem,
        compiler_params=pltpu.CompilerParams(vmem_limit_bytes=big),
        name="factor",
    )(summed)

    everyone = pl.pallas_call(
        functools.partial(gather_kernel, (core_bit, up, [core_bit] + owner)),
        out_shape=jax.ShapeDtypeStruct((*dims, PACK_ROWS, LANES), F32),
        in_specs=[vmem],
        out_specs=vmem,
        scratch_shapes=[
            pltpu.SemaphoreType.DMA((2, HEAD_BITS)),
            pltpu.SemaphoreType.DMA((2, HEAD_BITS)),
            pltpu.SemaphoreType.DMA((2, HEAD_BITS)),
            pltpu.SemaphoreType.DMA((2, HEAD_BITS)),
        ],
        compiler_params=pltpu.CompilerParams(
            collective_id=1, has_side_effects=True, vmem_limit_bytes=big
        ),
        name="gather",
    )(solved).reshape(HEADS, PACK_ROWS, LANES)

    piece_rows = width // tm
    place = lax.axis_index("tm").reshape(1).astype(jnp.int32)
    leverage, zscores, pieces = pl.pallas_call(
        functools.partial(leverage_kernel, scale),
        grid=(blocks,),
        in_specs=[
            pl.BlockSpec(memory_space=pltpu.SMEM),
            head_spec,
            feat_spec,
            line_spec,
            pl.BlockSpec((HEADS, PACK_ROWS, LANES), lambda b: (0, 0, 0)),
        ],
        out_specs=[
            line_spec,
            pl.BlockSpec((HEADS, width), lambda b: (0, 0)),
            pl.BlockSpec((HEADS, piece_rows, width), lambda b: (0, 0, 0)),
        ],
        out_shape=[
            jax.ShapeDtypeStruct((lines, LANES), F32),
            jax.ShapeDtypeStruct((HEADS, width), F32),
            jax.ShapeDtypeStruct((HEADS, piece_rows, width), F32),
        ],
        compiler_params=pltpu.CompilerParams(vmem_limit_bytes=big),
        name="leverage",
    )(place, heads, features, weights, everyone)
    return (leverage.reshape(row_count), zscores, pieces)


def solution(mesh):
    return jax.shard_map(
        functools.partial(local, dict(mesh.shape)),
        mesh=mesh,
        in_specs=(
            P(("station", "tm"), None),
            P(("station", "tm")),
            P(("station", "tm")),
            P(("station", "tm")),
            P("station", None),
        ),
        out_specs=(P(("station", "tm")), P(), P(None, "tm", None)),
        check_vma=False,
    )
```

time: 734 us -> 109 us (0.15)
  other arithmetic: 446 us -> 0 us
  waiting for transfers between devices: 170 us -> 0 us
  Pallas kernels: 0 us -> 105 us
  matrix products: 46.1 us -> 0 us
  blocking collectives: 35.8 us -> 0 us
  local copies, waits for them, and re-layouts: 20.3 us -> 3.09 us
  between operations: 14 us -> 0.69 us
    another operation x13 -> x0, other arithmetic: 429 us -> none  [the longest x9 269 us: factor_heads(): lower_factor = jnp.linalg.cholesky(gram_sum + identity)]
    pallas_call x0 -> x5, Pallas kernels: none -> 105 us  [the longest x1 36.1 us: local(): pl.pallas_call(functools.partial(reduce_kernel, (core_bit, down, [core_bi...]
    psum x1 -> x0, waiting for transfers between devices: 95.3 us -> none  [local(): share_gram, share_moment = lax.psum((share_gram, share_moment), 'tm')]
    reduce_scatter x2 -> x0, waiting for transfers between devices: 57.1 us -> none  [the longest x1 57.1 us: local(): lax.psum_scatter(gram_sum, 'station', scatter_dimension=0, tiled=True)]
    dot_general x9 -> x0, matrix products: 39.2 us -> none  [the longest x1 8.25 us: local(): jnp.einsum('bri,brj->bij', weight_blocks, feat_blocks, preferred_element_...]
    psum x1 -> x0, blocking collectives: 31 us -> none  [local(): share_gram, share_moment = lax.psum((share_gram, share_moment), 'tm')]
    all_gather x1 -> x0, waiting for transfers between devices: 17.4 us -> none  [local(): lax.all_gather(share_inverse, 'station', axis=0, tiled=True)]
    convert_element_type x2 -> x0, other arithmetic: 7.93 us -> none  [the longest x1 7.91 us: local(): weighted = (row_weight[:, None] * features).astype(jnp.bfloat16)]
  transfers between devices with their start and end apart: 4 -> 0, of which waited for: 3 -> 0; matrix products, arithmetic and copies ran while one was open for 63% -> 0% of each run, Pallas kernels for 0% -> 0%
where the time goes in v1:
time: 109 us; the launch traced here: 108 us
  Pallas kernels  105 us (96%)
  local copies, waits for them, and re-layouts  3.09 us (3%)
    pallas_call x1, Pallas kernels, local(): pl.pallas_call(functools.partial(reduce_kernel, (core_bit, down, [core_bi...  36.1 us
    pallas_call x1, Pallas kernels, local(): pl.pallas_call(functools.partial(gather_kernel, (core_bit, up, [core_bit]...  30.7 us
    pallas_call x1, Pallas kernels, local(): pl.pallas_call(gram_kernel, grid=(blocks,), in_specs=[head_spec, feat_spe...  14.9 us
    pallas_call x1, Pallas kernels, local(): pl.pallas_call(functools.partial(leverage_kernel, scale), grid=(blocks,),...  12.8 us
    pallas_call x1, Pallas kernels, local(): pl.pallas_call(factor_kernel, out_shape=jax.ShapeDtypeStruct((PACK_ROWS,...  10.2 us
    unnamed x10, local copies, waits for them, and re-layouts  3.09 us

profile of v1, /device:TPU:0, one launch (start us, length us, event | category | flops | bytes accessed | tf_op | source)
XLA Modules:
  0.0 108.5 jit_solution(1822119748620495955)
XLA Ops:
  0.6 0.0 copy-start
  0.6 0.8 copy-done
  1.5 0.0 copy-start.2
  1.5 0.8 copy-done.2
  2.3 0.0 copy-start.3
  2.3 0.8 copy-done.3
  3.1 0.0 copy-start.4
  3.1 0.7 copy-done.4
  3.7 14.9 %gram.1 = (f32[16,416,128]{2,1,0:T(8,128)S(1)}, f32[128,128]{1,0:T(8,128)S(1)}) custom-call(s32[128,128]{1,0:T(8,128)S(1)} %bitcast.9, bf16[16384,256]{1,0:T(8,128)(2,1)} %feat_ref.3, s32[128,128]{1,0:T(8,128)S(1)} %bitcast.11, bf16[128,128]{1,0:T(8,128)(2,1)S(1)} %bitcast.12, f32[1,128]{1,0:T(1,128)S(1)} %copy-done.4), custom_call_target="tpu_custom_call" | custom-call | tf_op jit(solution)/shard_map/gram/pallas_call | solution.py:326
  18.7 0.0 copy-start.1
  18.7 36.1 %reduce.1.g_ref = f32[416,128]{1,0:T(8,128)S(1)} custom-call(f32[2,2,2,2,416,128]{5,4,3,2,1,0:T(8,128)S(1)} %bitcast.8), custom_call_target="tpu_custom_call" | custom-call | tf_op jit(solution)/shard_map/reduce/pallas_call | solution.py:365
  54.8 10.2 %factor.1.x_ref = f32[416,128]{1,0:T(8,128)S(1)} custom-call(f32[416,128]{1,0:T(8,128)S(1)} %reduce.1.g_ref), custom_call_target="tpu_custom_call" | custom-call | tf_op jit(solution)/shard_map/factor/pallas_call | solution.py:384
  65.0 30.7 %gather.1 = f32[2,2,2,2,416,128]{5,4,3,2,1,0:T(8,128)S(1)} custom-call(f32[416,128]{1,0:T(8,128)S(1)} %factor.1.x_ref), custom_call_target="tpu_custom_call" | custom-call | tf_op jit(solution)/shard_map/gather/pallas_call | solution.py:393
  95.7 0.0 copy-done.1
  95.7 12.8 %leverage.1 = (f32[128,128]{1,0:T(8,128)}, f32[16,256]{1,0:T(8,128)}, f32[16,16,256]{2,1,0:T(8,128)}) custom-call(s32[1]{0:T(128)} %bitcast.place_ref, s32[128,128]{1,0:T(8,128)S(1)} %bitcast.10, bf16[16384,256]{1,0:T(8,128)(2,1)} %feat_ref.3, f32[128,128]{1,0:T(8,128)S(1)} %get-tuple-element.8.w_ref, f32[16,416,128]{2,1,0:T(8,128)S(1)} %bitcast.7), custom_call_target="tpu_custom_call" | custom-call | tf_op jit(solution)/shard_map/leverage/pallas_call | solution.py:412
Async XLA Ops:
  0.6 0.8 copy-start
  1.5 0.8 copy-start.2
  2.3 0.8 copy-start.3
  3.1 0.7 copy-start.4
  18.7 77.0 %copy-start.1 = (s32[16384]{0:T(1024)S(1)}, s32[16384]{0:T(1024)}, u32[]{:S(2)}) copy-start(s32[16384]{0:T(1024)} %param.8) | copy-start | bytes 196612

commit v2 on v1

v2 whole, which is shorter than its diff:
```python
import functools
import math

import jax
import jax.numpy as jnp
from jax import lax
from jax.experimental import pallas as pl
from jax.experimental.pallas import tpu as pltpu
from jax.sharding import PartitionSpec as P

HEADS = 16
BLK = 1024
LANES = 128
SUB = BLK // LANES
HEAD_BITS = 4
F32 = jnp.float32
HIGHEST = lax.Precision.HIGHEST
MESH = pl.DeviceIdType.MESH
PACK_ROWS = 336
VEC_ROW = 320
CHAINS = ((0, 48), (48, 40), (88, 40), (128, 40))


def bits_of(mesh_shape):
    station, tm = mesh_shape["station"], mesh_shape["tm"]
    core = ("tm", 1)
    owner = [("station", 1), ("tm", 2), ("tm", 4), ("tm", 8)]
    rest = [("station", s) for s in (2**i for i in range(1, 16)) if s < station]
    rest += [("tm", s) for s in (2**i for i in range(4, 16)) if s < tm]
    return core, owner, rest


def bit_value(bit):
    return lax.rem(lax.div(lax.axis_index(bit[0]), bit[1]), 2)


def partner(bit):
    axis, step = bit
    return {axis: lax.axis_index(axis) + (1 - 2 * bit_value(bit)) * step}


def greet(bits):
    barrier = pltpu.get_barrier_semaphore()
    for bit in bits:
        pl.semaphore_signal(barrier, inc=1, device_id=partner(bit), device_id_type=MESH)
    pl.semaphore_wait(barrier, len(bits))


def half_tiles(full):
    return full[64:128, :], full[0:64, :]


def gram_kernel(
    heads_hbm, feat_ref, ids_hbm, tgt_hbm, table_hbm, out_ref, w_ref, acc, vec, heads, ids, low, tgt, table, sems
):
    step = pl.program_id(0)
    per = feat_ref.shape[0] // BLK

    @pl.when(step == 0)
    def _():
        copies = [
            pltpu.make_async_copy(src, dst, sems.at[i])
            for i, (src, dst) in enumerate(
                ((ids_hbm, ids), (table_hbm, table), (tgt_hbm, low), (heads_hbm, heads))
            )
        ]
        for copy in copies:
            copy.start()
        acc[...] = jnp.zeros_like(acc)
        vec[...] = jnp.zeros_like(vec)
        for copy in copies:
            copy.wait()
        tgt[...] = low[...].astype(F32)

    lookup = jnp.broadcast_to(table[...], (SUB, LANES))
    row = lax.broadcasted_iota(jnp.int32, (SUB, LANES), 0)
    for i in range(per):
        line = pl.multiple_of((step * per + i) * SUB, SUB)
        weights = jnp.take_along_axis(
            lookup, ids[pl.ds(line, SUB), :], axis=1, mode="promise_in_bounds"
        )
        w_ref[i * SUB : (i + 1) * SUB, :] = weights
        feat = feat_ref[i * BLK : (i + 1) * BLK, :]
        turned = feat.T
        scaled = jnp.concatenate(
            [
                (turned[:, c * LANES : (c + 1) * LANES].astype(F32) * weights[c : c + 1, :]).astype(
                    jnp.bfloat16
                )
                for c in range(SUB)
            ],
            axis=1,
        )
        head = heads[line, 0]
        acc[head] += jnp.dot(scaled, feat, preferred_element_type=F32)
        here = tgt[pl.ds(line, SUB), :]
        spread = jnp.concatenate([jnp.where(row == c, here, 0.0) for c in range(SUB)], axis=1)
        vec[head] += lax.dot_general(
            spread.astype(jnp.bfloat16),
            scaled,
            (((1,), (1,)), ((), ())),
            preferred_element_type=F32,
        )

    @pl.when(step == pl.num_programs(0) - 1)
    def _():
        left = lax.broadcasted_iota(jnp.int32, (64, LANES), 1) < 64

        @pl.loop(0, HEADS)
        def _(h):
            g11, g22 = acc[h, 0:128, 0:128], acc[h, 128:256, 128:256]
            lower1, top1 = half_tiles(0.5 * (g11 + g11.T))
            lower2, top2 = half_tiles(0.5 * (g22 + g22.T))
            out_ref[h, 0:64, :] = jnp.where(left, top1, pltpu.roll(top2, 64, 1))
            out_ref[h, 64:128, :] = lower1
            out_ref[h, 128:192, :] = lower2
            out_ref[h, 192:320, :] = 0.5 * (acc[h, 128:256, 0:128] + acc[h, 0:128, 128:256].T)
            total = jnp.sum(vec[h], axis=0, keepdims=True)
            out_ref[h, VEC_ROW:PACK_ROWS, :] = jnp.zeros((PACK_ROWS - VEC_ROW, LANES), F32)
            out_ref[h, VEC_ROW : VEC_ROW + 1, :] = total[:, 0:128]
            out_ref[h, VEC_ROW + 1 : VEC_ROW + 2, :] = total[:, 128:256]


def reduce_kernel(plan, g_ref, out_ref, acc, first, fin, *rest):
    core_bit, orders, all_bits = plan
    stage_count = len(orders[0])
    count = len(CHAINS)
    bufs = [rest[c * stage_count : (c + 1) * stage_count] for c in range(count)]
    send, recv = rest[-2:]
    half = PACK_ROWS // 2
    core = bit_value(core_bit)
    own = [pl.ds(start, size) for start, size in CHAINS]
    mine = [pl.ds(pl.multiple_of(core * half + start, 8), size) for start, size in CHAINS]
    theirs = [pl.ds(pl.multiple_of((1 - core) * half + start, 8), size) for start, size in CHAINS]
    greet(all_bits)
    sent = []
    flying = [None] * count
    index = [[slice(None)] * HEAD_BITS for _ in range(count)]

    def push(src, dst, chain, stage, bit):
        copy = pltpu.make_async_remote_copy(
            src_ref=src,
            dst_ref=dst,
            send_sem=send.at[chain, stage],
            recv_sem=recv.at[chain, stage],
            device_id=partner(bit),
            device_id_type=MESH,
        )
        copy.start()
        sent.append(copy)
        flying[chain] = copy

    def take(c, stage):
        flying[c].wait_recv()
        place = (*index[c], own[c])
        if stage == 0:
            acc[place] = g_ref[:, :, :, :, mine[c], :] + first[place]
        else:
            acc[place] = acc[place] + bufs[c][stage - 1][...]

    def give(c, stage):
        if stage == stage_count:
            push(acc.at[(*index[c], own[c])], fin.at[own[c]], c, stage + 1, core_bit)
            return
        bit, dim = orders[c % 2][stage]
        away = list(index[c])
        if dim is not None:
            away[dim] = 1 - bit_value(bit)
            index[c][dim] = bit_value(bit)
        push(acc.at[(*away, own[c])], bufs[c][stage], c, stage + 1, bit)

    every = [slice(None)] * HEAD_BITS
    for c in range(count):
        push(g_ref.at[(*every, theirs[c])], first.at[(*every, own[c])], c, 0, core_bit)
    ahead, behind = (0, 1), (2, 3)
    for c in ahead:
        take(c, 0)
        give(c, 0)
    for c in behind:
        take(c, 0)
    for stage in range(1, stage_count + 1):
        for c in ahead:
            take(c, stage)
            give(c, stage)
        for c in behind:
            if stage > 1:
                take(c, stage - 1)
            give(c, stage - 1)
    for c in behind:
        take(c, stage_count)
        give(c, stage_count)
    for c in range(count):
        flying[c].wait_recv()
        out_ref[mine[c], :] = acc[(*index[c], own[c])]
        out_ref[theirs[c], :] = fin[own[c], :]
    for copy in sent:
        copy.wait_send()


def gather_kernel(plan, x_ref, out_ref, send, recv, send_core, recv_core):
    core_bit, orders, all_bits = plan
    count = len(CHAINS)
    half = PACK_ROWS // 2
    core = bit_value(core_bit)
    mine = [pl.ds(pl.multiple_of(core * half + start, 8), size) for start, size in CHAINS]
    own = [None] * HEAD_BITS
    for bit, dim in orders[0]:
        own[dim] = bit_value(bit)
    out_ref[(*own,)] = x_ref[...]
    greet(all_bits)
    sent, late = [], []

    def push(place, chain, bit, send_sem, recv_sem):
        view = out_ref.at[(*place, mine[chain])]
        copy = pltpu.make_async_remote_copy(
            src_ref=view,
            dst_ref=view,
            send_sem=send_sem,
            recv_sem=recv_sem,
            device_id=partner(bit),
            device_id_type=MESH,
        )
        copy.start()
        sent.append(copy)
        return copy

    index = [list(own) for _ in range(count)]
    flying = [None] * count

    def give(c, stage):
        if stage < HEAD_BITS:
            bit, dim = orders[c % 2][stage]
            flying[c] = push(index[c], c, bit, send.at[c, stage], recv.at[c, stage])

    def take(c, stage):
        flying[c].wait_recv()
        bit, dim = orders[c % 2][stage]
        news = list(index[c])
        news[dim] = 1 - bit_value(bit)
        index[c][dim] = slice(None)
        give(c, stage + 1)
        late.append(push(news, c, core_bit, send_core.at[c, stage], recv_core.at[c, stage]))

    ahead, behind = (0, 1), (2, 3)
    for c in ahead:
        give(c, 0)
    for stage in range(HEAD_BITS + 2):
        for c in ahead:
            if stage < HEAD_BITS:
                take(c, stage)
        for c in behind:
            if stage == 1:
                give(c, 0)
            if stage >= 2:
                take(c, stage - 2)
    for copy in late:
        copy.wait_recv()
    for copy in sent:
        copy.wait_send()


def mm(a, b, dims):
    return lax.dot_general(a, b, (dims, ((), ())), precision=HIGHEST, preferred_element_type=F32)


def eliminate(matrix, offset):
    groups = matrix.shape[0] // 8
    rows = [matrix[8 * g : 8 * g + 8, :] for g in range(groups)]
    below = lax.broadcasted_iota(jnp.int32, (8, LANES), 0)
    for p in range(groups):
        columns = [offset + 8 * p + k for k in range(8)]
        pivots = [None] * 8
        across = [[None] * 8 for _ in range(8)]
        lines = [None] * 8
        for g in range(p, groups):
            cols = [jnp.broadcast_to(rows[g][:, j : j + 1], (8, LANES)) for j in columns]
            for k in range(8):
                if g == p:
                    pivots[k] = 1.0 / cols[k][k : k + 1, :]
                    lines[k] = rows[p][k : k + 1, :]
                    for m in range(k + 1, 8):
                        across[k][m] = cols[m][k : k + 1, :]
                factor = cols[k] * pivots[k]
                if g == p:
                    factor = jnp.where(below > k, factor, 0.0)
                for m in range(k + 1, 8):
                    cols[m] = cols[m] - factor * across[k][m]
                rows[g] = rows[g] - factor * lines[k]
    done = jnp.concatenate(rows, axis=0)
    lane = lax.broadcasted_iota(jnp.int32, done.shape, 1)
    row = lax.broadcasted_iota(jnp.int32, done.shape, 0)
    diagonal = jnp.sum(jnp.where(lane == row + offset, done, 0.0), axis=1, keepdims=True)
    return done * (1.0 / jnp.sqrt(diagonal))


def inverse_factor_128(top, bottom):
    lane = lax.broadcasted_iota(jnp.int32, (64, LANES), 1)
    row = lax.broadcasted_iota(jnp.int32, (64, LANES), 0)
    low = lane < 64
    eye = (lane == row + 64).astype(F32)
    none = jnp.zeros((64, LANES), F32)
    first = eliminate(jnp.where(low, top, eye), 0)
    x1 = jnp.where(low, pltpu.roll(first, 64, 1), 0.0)
    x1_full = jnp.concatenate([x1, none], axis=0)
    lower = mm(bottom, x1_full, ((1,), (1,)))
    square = mm(lower, jnp.concatenate([lower, none], axis=0), ((1,), (1,)))
    second = eliminate(jnp.where(low, pltpu.roll(bottom, 64, 1) - square, eye), 0)
    x2 = jnp.where(low, 0.0, second)
    across = mm(lower, x1_full, ((1,), (0,)))
    x21 = -mm(x2, jnp.concatenate([none, across], axis=0), ((1,), (0,)))
    return x1, x21 + x2


def factor_kernel(g_ref, out_ref):
    lane = lax.broadcasted_iota(jnp.int32, (64, LANES), 1)
    row = lax.broadcasted_iota(jnp.int32, (64, LANES), 0)
    low = lane < 64
    eye_top = (lane == row).astype(F32)
    eye_bottom = (lane == row + 64).astype(F32)
    tops = g_ref[0:64, :]
    top1, bottom1 = inverse_factor_128(tops + eye_top, g_ref[64:128, :] + eye_bottom)
    x1 = jnp.concatenate([top1, bottom1], axis=0)
    lower = mm(g_ref[192:320, :], x1, ((1,), (1,)))
    square = mm(lower, lower, ((1,), (1,)))
    top2, bottom2 = inverse_factor_128(
        pltpu.roll(tops, 64, 1) + eye_top - square[0:64, :],
        g_ref[128:192, :] + eye_bottom - square[64:128, :],
    )
    x2 = jnp.concatenate([top2, bottom2], axis=0)
    x21 = -mm(x2, mm(lower, x1, ((1,), (0,))), ((1,), (0,)))
    out_ref[0:64, :] = jnp.where(low, top1, pltpu.roll(top2, 64, 1))
    out_ref[64:128, :] = bottom1
    out_ref[128:192, :] = bottom2
    out_ref[192:320, :] = x21
    m1 = jnp.broadcast_to(g_ref[VEC_ROW : VEC_ROW + 1, :], (8, LANES))
    m2 = jnp.broadcast_to(g_ref[VEC_ROW + 1 : VEC_ROW + 2, :], (8, LANES))
    in1 = mm(m1, x1, ((1,), (1,)))
    in2 = mm(m1, x21, ((1,), (1,))) + mm(m2, x2, ((1,), (1,)))
    co1 = mm(in1, x1, ((1,), (0,))) + mm(in2, x21, ((1,), (0,)))
    co2 = mm(in2, x2, ((1,), (0,)))
    s1 = jnp.sum(x1 * x1, axis=0, keepdims=True) + jnp.sum(x21 * x21, axis=0, keepdims=True)
    s2 = jnp.sum(x2 * x2, axis=0, keepdims=True)
    out_ref[VEC_ROW:PACK_ROWS, :] = jnp.zeros((PACK_ROWS - VEC_ROW, LANES), F32)
    out_ref[VEC_ROW : VEC_ROW + 1, :] = co1[0:1, :] / jnp.sqrt(s1)
    out_ref[VEC_ROW + 1 : VEC_ROW + 2, :] = co2[0:1, :] / jnp.sqrt(s2)


def leverage_kernel(scale, place_ref, heads_ref, feat_ref, w_ref, inv_ref, lev_ref, z_ref, piece_ref):
    step = pl.program_id(0)
    per = feat_ref.shape[0] // BLK

    @pl.when(step == 0)
    def _():
        z_ref[:, 0:128] = inv_ref[:, VEC_ROW, :]
        z_ref[:, 128:256] = inv_ref[:, VEC_ROW + 1, :]
        count = piece_ref.shape[1]
        start = place_ref[0] * count
        root = math.sqrt(scale * 2 * LANES)
        low = lax.broadcasted_iota(jnp.int32, (count, LANES), 1) < 64

        def rows(first):
            return inv_ref[:, pl.ds(pl.multiple_of(first, 8), count), :] * root

        @pl.when(start < 64)
        def _():
            piece_ref[:, :, 0:128] = jnp.where(low, rows(start), 0.0)

        @pl.when(jnp.logical_and(start >= 64, start < 128))
        def _():
            piece_ref[:, :, 0:128] = rows(start)

        @pl.when(start < 128)
        def _():
            piece_ref[:, :, 128:256] = jnp.zeros((HEADS, count, LANES), F32)

        @pl.when(start >= 128)
        def _():
            piece_ref[:, :, 0:128] = rows(start + 64)

        @pl.when(jnp.logical_and(start >= 128, start < 192))
        def _():
            for h in range(HEADS):
                part = inv_ref[h, pl.ds(pl.multiple_of(start - 128, 8), count), :] * root
                piece_ref[h, :, 128:256] = jnp.where(low, pltpu.roll(part, 64, 1), 0.0)

        @pl.when(start >= 192)
        def _():
            piece_ref[:, :, 128:256] = rows(start - 64)

    low = lax.broadcasted_iota(jnp.int32, (64, LANES), 1) < 64
    zero = jnp.zeros((128, 128), jnp.bfloat16)
    for i in range(per):
        head = heads_ref[i * SUB, 0]
        tops = inv_ref[head, 0:64, :]
        x1 = jnp.concatenate([jnp.where(low, tops, 0.0), inv_ref[head, 64:128, :]], axis=0)
        x2 = jnp.concatenate(
            [jnp.where(low, pltpu.roll(tops, 64, 1), 0.0), inv_ref[head, 128:192, :]], axis=0
        )
        x21 = inv_ref[head, 192:320, :]
        x1, x21, x2 = (x.astype(jnp.bfloat16) for x in (x1, x21, x2))
        inverse = jnp.concatenate(
            [jnp.concatenate([x1, zero], axis=1), jnp.concatenate([x21, x2], axis=1)], axis=0
        )
        projected = lax.dot_general(
            feat_ref[i * BLK : (i + 1) * BLK, :],
            inverse,
            (((1,), (1,)), ((), ())),
            preferred_element_type=F32,
        )
        one, two = projected[:, 0:128], projected[:, 128:256]
        squares = one * one + two * two
        for c in range(SUB):
            line = jnp.sum(squares[c * LANES : (c + 1) * LANES, :].T, axis=0, keepdims=True)
            here = i * SUB + c
            lev_ref[here : here + 1, :] = w_ref[here : here + 1, :] * line * scale


def local(mesh_shape, features, targets, station_ids, lead_heads, station_weight):
    row_count, width = features.shape
    blocks = row_count // BLK
    lines = row_count // LANES
    tm = mesh_shape["tm"]
    total_rows = row_count * mesh_shape["station"] * tm
    scale = total_rows / (HEADS * width)
    ids = station_ids.reshape(lines, LANES)
    heads = lead_heads.reshape(lines, LANES)
    goals = targets.reshape(lines, LANES)
    per = math.gcd(blocks, 4)
    head_spec = pl.BlockSpec((per * SUB, LANES), lambda b: (b, 0), memory_space=pltpu.SMEM)
    line_spec = pl.BlockSpec((per * SUB, LANES), lambda b: (b, 0))
    feat_spec = pl.BlockSpec((per * BLK, width), lambda b: (b, 0))
    away = pl.BlockSpec(memory_space=pltpu.HBM)
    big = 48 * 1024 * 1024
    packed, weights = pl.pallas_call(
        gram_kernel,
        grid=(blocks // per,),
        in_specs=[
            away,
            feat_spec,
            away,
            away,
            away,
        ],
        out_specs=[pl.BlockSpec((HEADS, PACK_ROWS, LANES), lambda b: (0, 0, 0)), line_spec],
        out_shape=[
            jax.ShapeDtypeStruct((HEADS, PACK_ROWS, LANES), F32),
            jax.ShapeDtypeStruct((lines, LANES), F32),
        ],
        scratch_shapes=[
            pltpu.VMEM((HEADS, width, width), F32),
            pltpu.VMEM((HEADS, 8, width), F32),
            pltpu.SMEM((lines, LANES), jnp.int32),
            pltpu.VMEM((lines, LANES), jnp.int32),
            pltpu.VMEM((lines, LANES), jnp.bfloat16),
            pltpu.VMEM((lines, LANES), F32),
            pltpu.VMEM(station_weight.shape, F32),
            pltpu.SemaphoreType.DMA((4,)),
        ],
        compiler_params=pltpu.CompilerParams(vmem_limit_bytes=big),
        name="gram",
    )(heads, features, ids, goals, station_weight)

    core_bit, owner, rest = bits_of(mesh_shape)
    named = [(bit, dim) for dim, bit in enumerate(owner)]
    x, y, z0, z1 = named
    tail = [(bit, None) for bit in rest]
    down = ([x, y, z0, z1] + tail, [y, x, z0, z1] + tail)
    up = ([z1, z0, y, x], [z1, z0, x, y])
    dims = (2,) * HEAD_BITS
    half = PACK_ROWS // 2
    count = len(CHAINS)
    buffers = []
    for c, (_, size) in enumerate(CHAINS):
        free = HEAD_BITS
        for bit, dim in down[c % 2]:
            free -= dim is not None
            buffers.append(pltpu.VMEM((2,) * free + (size, LANES), F32))
    vmem = pl.BlockSpec(memory_space=pltpu.VMEM)
    summed = pl.pallas_call(
        functools.partial(reduce_kernel, (core_bit, down, [core_bit] + owner + rest)),
        out_shape=jax.ShapeDtypeStruct((PACK_ROWS, LANES), F32),
        in_specs=[vmem],
        out_specs=vmem,
        scratch_shapes=[
            pltpu.VMEM((*dims, half, LANES), F32),
            pltpu.VMEM((*dims, half, LANES), F32),
            pltpu.VMEM((half, LANES), F32),
            *buffers,
            pltpu.SemaphoreType.DMA((count, len(down[0]) + 2)),
            pltpu.SemaphoreType.DMA((count, len(down[0]) + 2)),
        ],
        compiler_params=pltpu.CompilerParams(
            collective_id=0, has_side_effects=True, vmem_limit_bytes=big
        ),
        name="reduce",
    )(packed.reshape(*dims, PACK_ROWS, LANES))

    solved = pl.pallas_call(
        factor_kernel,
        out_shape=jax.ShapeDtypeStruct((PACK_ROWS, LANES), F32),
        in_specs=[vmem],
        out_specs=vmem,
        compiler_params=pltpu.CompilerParams(vmem_limit_bytes=big),
        name="factor",
    )(summed)

    everyone = pl.pallas_call(
        functools.partial(gather_kernel, (core_bit, up, [core_bit] + owner)),
        out_shape=jax.ShapeDtypeStruct((*dims, PACK_ROWS, LANES), F32),
        in_specs=[vmem],
        out_specs=vmem,
        scratch_shapes=[
            pltpu.SemaphoreType.DMA((count, HEAD_BITS)),
            pltpu.SemaphoreType.DMA((count, HEAD_BITS)),
            pltpu.SemaphoreType.DMA((count, HEAD_BITS)),
            pltpu.SemaphoreType.DMA((count, HEAD_BITS)),
        ],
        compiler_params=pltpu.CompilerParams(
            collective_id=1, has_side_effects=True, vmem_limit_bytes=big
        ),
        name="gather",
    )(solved).reshape(HEADS, PACK_ROWS, LANES)

    piece_rows = width // tm
    place = lax.axis_index("tm").reshape(1).astype(jnp.int32)
    leverage, zscores, pieces = pl.pallas_call(
        functools.partial(leverage_kernel, scale),
        grid=(blocks // per,),
        in_specs=[
            pl.BlockSpec(memory_space=pltpu.SMEM),
            head_spec,
            feat_spec,
            line_spec,
            pl.BlockSpec((HEADS, PACK_ROWS, LANES), lambda b: (0, 0, 0)),
        ],
        out_specs=[
            line_spec,
            pl.BlockSpec((HEADS, width), lambda b: (0, 0)),
            pl.BlockSpec((HEADS, piece_rows, width), lambda b: (0, 0, 0)),
        ],
        out_shape=[
            jax.ShapeDtypeStruct((lines, LANES), F32),
            jax.ShapeDtypeStruct((HEADS, width), F32),
            jax.ShapeDtypeStruct((HEADS, piece_rows, width), F32),
        ],
        compiler_params=pltpu.CompilerParams(vmem_limit_bytes=big),
        name="leverage",
    )(place, heads, features, weights, everyone)
    return (leverage.reshape(row_count), zscores, pieces)


def solution(mesh):
    return jax.shard_map(
        functools.partial(local, dict(mesh.shape)),
        mesh=mesh,
        in_specs=(
            P(("station", "tm"), None),
            P(("station", "tm")),
            P(("station", "tm")),
            P(("station", "tm")),
            P("station", None),
        ),
        out_specs=(P(("station", "tm")), P(), P(None, "tm", None)),
        check_vma=False,
    )
```

time: 109 us -> 91.6 us (0.84)
  Pallas kernels: 105 us -> 87 us
    pallas_call x2, Pallas kernels: 27.7 us -> 18.2 us  [the longest x1 11.4 us: local(): pl.pallas_call(gram_kernel, grid=(blocks // per,), in_specs=[away, feat_s...]
    pallas_call x1, Pallas kernels: 36.1 us -> 31.6 us  [local(): pl.pallas_call(functools.partial(reduce_kernel, (core_bit, down, [core_bi...]
    pallas_call x1, Pallas kernels: 30.7 us -> 27.1 us  [local(): pl.pallas_call(functools.partial(gather_kernel, (core_bit, up, [core_bit]...]
where the time goes in v2:
time: 91.6 us; the launch traced here: 90.8 us
  Pallas kernels  87 us (95%)
  local copies, waits for them, and re-layouts  3.09 us (3%)
    pallas_call x1, Pallas kernels, local(): pl.pallas_call(functools.partial(reduce_kernel, (core_bit, down, [core_bi...  31.6 us
    pallas_call x1, Pallas kernels, local(): pl.pallas_call(functools.partial(gather_kernel, (core_bit, up, [core_bit]...  27.1 us
    pallas_call x1, Pallas kernels, local(): pl.pallas_call(gram_kernel, grid=(blocks // per,), in_specs=[away, feat_s...  11.4 us
    pallas_call x1, Pallas kernels, local(): pl.pallas_call(factor_kernel, out_shape=jax.ShapeDtypeStruct((PACK_ROWS,...  10.1 us
    pallas_call x1, Pallas kernels, local(): pl.pallas_call(functools.partial(leverage_kernel, scale), grid=(blocks //...  6.8 us
    unnamed x10, local copies, waits for them, and re-layouts  3.09 us

profile of v2, /device:TPU:0, one launch (start us, length us, event | category | flops | bytes accessed | tf_op | source)
XLA Modules:
  0.0 90.8 jit_solution(4029836623441502626)
XLA Ops:
  0.6 0.0 copy-start
  0.6 0.8 copy-done
  1.5 0.0 copy-start.2
  1.5 0.8 copy-done.2
  2.3 0.0 copy-start.3
  2.3 0.8 copy-done.3
  3.1 0.0 copy-start.4
  3.1 0.7 copy-done.4
  3.7 11.4 %gram.1 = (f32[16,336,128]{2,1,0:T(8,128)S(1)}, f32[128,128]{1,0:T(8,128)S(1)}) custom-call(s32[128,128]{1,0:T(8,128)S(1)} %bitcast.9, bf16[16384,256]{1,0:T(8,128)(2,1)} %feat_ref.3, s32[128,128]{1,0:T(8,128)S(1)} %bitcast.11, bf16[128,128]{1,0:T(8,128)(2,1)S(1)} %bitcast.12, f32[1,128]{1,0:T(1,128)S(1)} %copy-done.4), custom_call_target="tpu_custom_call" | custom-call | tf_op jit(solution)/shard_map/gram/pallas_call | solution.py:434
  15.1 0.0 copy-start.1
  15.2 31.6 %reduce.1.g_ref = f32[336,128]{1,0:T(8,128)S(1)} custom-call(f32[2,2,2,2,336,128]{5,4,3,2,1,0:T(8,128)S(1)} %bitcast.8), custom_call_target="tpu_custom_call" | custom-call | tf_op jit(solution)/shard_map/reduce/pallas_call | solution.py:479
  46.8 10.1 %factor.1.x_ref = f32[336,128]{1,0:T(8,128)S(1)} custom-call(f32[336,128]{1,0:T(8,128)S(1)} %reduce.1.g_ref), custom_call_target="tpu_custom_call" | custom-call | tf_op jit(solution)/shard_map/factor/pallas_call | solution.py:498
  56.9 27.1 %gather.1 = f32[2,2,2,2,336,128]{5,4,3,2,1,0:T(8,128)S(1)} custom-call(f32[336,128]{1,0:T(8,128)S(1)} %factor.1.x_ref), custom_call_target="tpu_custom_call" | custom-call | tf_op jit(solution)/shard_map/gather/pallas_call | solution.py:507
  84.0 0.0 copy-done.1
  84.0 6.8 %leverage.1 = (f32[128,128]{1,0:T(8,128)}, f32[16,256]{1,0:T(8,128)}, f32[16,16,256]{2,1,0:T(8,128)}) custom-call(s32[1]{0:T(128)} %bitcast.place_ref, s32[128,128]{1,0:T(8,128)S(1)} %bitcast.10, bf16[16384,256]{1,0:T(8,128)(2,1)} %feat_ref.3, f32[128,128]{1,0:T(8,128)S(1)} %get-tuple-element.8.w_ref, f32[16,336,128]{2,1,0:T(8,128)S(1)} %bitcast.7), custom_call_target="tpu_custom_call" | custom-call | tf_op jit(solution)/shard_map/leverage/pallas_call | solution.py:526
Async XLA Ops:
  0.6 0.8 copy-start
  1.5 0.8 copy-start.2
  2.3 0.8 copy-start.3
  3.1 0.7 copy-start.4
  15.1 68.8 %copy-start.1 = (s32[16384]{0:T(1024)S(1)}, s32[16384]{0:T(1024)}, u32[]{:S(2)}) copy-start(s32[16384]{0:T(1024)} %param.8) | copy-start | bytes 196612

commit v3 on v2

--- a/solution.py
+++ b/solution.py
@@ -18,7 +18,7 @@
 MESH = pl.DeviceIdType.MESH
 PACK_ROWS = 336
 VEC_ROW = 320
-CHAINS = ((0, 48), (48, 40), (88, 40), (128, 40))
+CHAINS = ((0, 32), (32, 32), (64, 56), (120, 48))
 
 
 def bits_of(mesh_shape):
@@ -34,16 +34,34 @@
     return lax.rem(lax.div(lax.axis_index(bit[0]), bit[1]), 2)
 
 
-def partner(bit):
-    axis, step = bit
-    return {axis: lax.axis_index(axis) + (1 - 2 * bit_value(bit)) * step}
-
-
-def greet(bits):
+def moves_of(bits):
+    return range(1, 2 ** len(bits))
+
+
+def partner(bits, move):
+    place = {}
+    for i, (axis, step) in enumerate(bits):
+        if (move >> i) & 1:
+            here = place.get(axis, lax.axis_index(axis))
+            place[axis] = here + (1 - 2 * bit_value((axis, step))) * step
+    return place
+
+
+def flipped(bit, i, move):
+    value = bit_value(bit)
+    return 1 - value if (move >> i) & 1 else value
+
+
+def greet(groups):
     barrier = pltpu.get_barrier_semaphore()
-    for bit in bits:
-        pl.semaphore_signal(barrier, inc=1, device_id=partner(bit), device_id_type=MESH)
-    pl.semaphore_wait(barrier, len(bits))
+    met = 0
+    for bits in groups:
+        for move in moves_of(bits):
+            pl.semaphore_signal(
+                barrier, inc=1, device_id=partner(bits, move), device_id_type=MESH
+            )
+            met += 1
+    pl.semaphore_wait(barrier, met)
 
 
 def half_tiles(full):
@@ -106,7 +124,7 @@
     def _():
         left = lax.broadcasted_iota(jnp.int32, (64, LANES), 1) < 64
 
-        @pl.loop(0, HEADS)
+        @pl.loop(0, HEADS, unroll=4)
         def _(h):
             g11, g22 = acc[h, 0:128, 0:128], acc[h, 128:256, 128:256]
             lower1, top1 = half_tiles(0.5 * (g11 + g11.T))
@@ -122,75 +140,72 @@
 
 
 def reduce_kernel(plan, g_ref, out_ref, acc, first, fin, *rest):
-    core_bit, orders, all_bits = plan
+    core_bits, orders, groups = plan
     stage_count = len(orders[0])
     count = len(CHAINS)
     bufs = [rest[c * stage_count : (c + 1) * stage_count] for c in range(count)]
     send, recv = rest[-2:]
     half = PACK_ROWS // 2
-    core = bit_value(core_bit)
+    core = bit_value(core_bits[0])
     own = [pl.ds(start, size) for start, size in CHAINS]
     mine = [pl.ds(pl.multiple_of(core * half + start, 8), size) for start, size in CHAINS]
     theirs = [pl.ds(pl.multiple_of((1 - core) * half + start, 8), size) for start, size in CHAINS]
-    greet(all_bits)
+    greet(groups)
     sent = []
-    flying = [None] * count
+    flying = [[] for _ in range(count)]
     index = [[slice(None)] * HEAD_BITS for _ in range(count)]
 
-    def push(src, dst, chain, stage, bit):
+    def push(src, dst, chain, stage, bits, move):
         copy = pltpu.make_async_remote_copy(
             src_ref=src,
             dst_ref=dst,
-            send_sem=send.at[chain, stage],
-            recv_sem=recv.at[chain, stage],
-            device_id=partner(bit),
+            send_sem=send.at[chain, stage, move - 1],
+            recv_sem=recv.at[chain, stage, move - 1],
+            device_id=partner(bits, move),
             device_id_type=MESH,
         )
         copy.start()
         sent.append(copy)
-        flying[chain] = copy
+        flying[chain].append(copy)
 
     def take(c, stage):
-        flying[c].wait_recv()
+        arrived, flying[c] = flying[c], []
         place = (*index[c], own[c])
-        if stage == 0:
-            acc[place] = g_ref[:, :, :, :, mine[c], :] + first[place]
-        else:
-            acc[place] = acc[place] + bufs[c][stage - 1][...]
+        for i, copy in enumerate(arrived):
+            copy.wait_recv()
+            if stage > 0 and not orders[c % 2][stage - 1][1]:
+                copy.wait_send()
+                sent[:] = [other for other in sent if other is not copy]
+            if stage == 0:
+                acc[place] = g_ref[:, :, :, :, mine[c], :] + first[place]
+            else:
+                acc[place] = acc[place] + bufs[c][stage - 1][i]
 
     def give(c, stage):
         if stage == stage_count:
-            push(acc.at[(*index[c], own[c])], fin.at[own[c]], c, stage + 1, core_bit)
+            push(acc.at[(*index[c], own[c])], fin.at[own[c]], c, stage + 1, core_bits, 1)
             return
-        bit, dim = orders[c % 2][stage]
-        away = list(index[c])
-        if dim is not None:
-            away[dim] = 1 - bit_value(bit)
-            index[c][dim] = bit_value(bit)
-        push(acc.at[(*away, own[c])], bufs[c][stage], c, stage + 1, bit)
+        bits, dims = orders[c % 2][stage]
+        kept = list(index[c])
+        for move in reversed(moves_of(bits)):
+            away = list(index[c])
+            for i, dim in enumerate(dims):
+                away[dim] = flipped(bits[i], i, move)
+                kept[dim] = bit_value(bits[i])
+            push(acc.at[(*away, own[c])], bufs[c][stage].at[move - 1], c, stage + 1, bits, move)
+        flying[c].reverse()
+        index[c] = kept
 
     every = [slice(None)] * HEAD_BITS
     for c in range(count):
-        push(g_ref.at[(*every, theirs[c])], first.at[(*every, own[c])], c, 0, core_bit)
-    ahead, behind = (0, 1), (2, 3)
-    for c in ahead:
-        take(c, 0)
-        give(c, 0)
-    for c in behind:
-        take(c, 0)
-    for stage in range(1, stage_count + 1):
-        for c in ahead:
+        push(g_ref.at[(*every, theirs[c])], first.at[(*every, own[c])], c, 0, core_bits, 1)
+    for stage in range(stage_count + 1):
+        for c in range(count):
             take(c, stage)
             give(c, stage)
-        for c in behind:
-            if stage > 1:
-                take(c, stage - 1)
-            give(c, stage - 1)
-    for c in behind:
-        take(c, stage_count)
-        give(c, stage_count)
     for c in range(count):
-        flying[c].wait_recv()
+        for copy in flying[c]:
+            copy.wait_recv()
         out_ref[mine[c], :] = acc[(*index[c], own[c])]
         out_ref[theirs[c], :] = fin[own[c], :]
     for copy in sent:
@@ -198,26 +213,27 @@
 
 
 def gather_kernel(plan, x_ref, out_ref, send, recv, send_core, recv_core):
-    core_bit, orders, all_bits = plan
+    core_bits, orders, groups = plan
     count = len(CHAINS)
     half = PACK_ROWS // 2
-    core = bit_value(core_bit)
+    core = bit_value(core_bits[0])
     mine = [pl.ds(pl.multiple_of(core * half + start, 8), size) for start, size in CHAINS]
     own = [None] * HEAD_BITS
-    for bit, dim in orders[0]:
-        own[dim] = bit_value(bit)
+    for bits, dims in orders[0]:
+        for bit, dim in zip(bits, dims):
+            own[dim] = bit_value(bit)
     out_ref[(*own,)] = x_ref[...]
-    greet(all_bits)
+    greet(groups)
     sent, late = [], []
 
-    def push(place, chain, bit, send_sem, recv_sem):
+    def push(place, chain, bits, move, send_sem, recv_sem):
         view = out_ref.at[(*place, mine[chain])]
         copy = pltpu.make_async_remote_copy(
             src_ref=view,
             dst_ref=view,
             send_sem=send_sem,
             recv_sem=recv_sem,
-            device_id=partner(bit),
+            device_id=partner(bits, move),
             device_id_type=MESH,
         )
         copy.start()
@@ -225,34 +241,57 @@
         return copy
 
     index = [list(own) for _ in range(count)]
-    flying = [None] * count
+    flying = [[] for _ in range(count)]
+    stage_count = len(orders[0])
 
     def give(c, stage):
-        if stage < HEAD_BITS:
-            bit, dim = orders[c % 2][stage]
-            flying[c] = push(index[c], c, bit, send.at[c, stage], recv.at[c, stage])
+        if stage < stage_count:
+            bits, dims = orders[c % 2][stage]
+            flying[c] = [
+                (
+                    move,
+                    push(
+                        index[c],
+                        c,
+                        bits,
+                        move,
+                        send.at[c, stage, move - 1],
+                        recv.at[c, stage, move - 1],
+                    ),
+                )
+                for move in reversed(moves_of(bits))
+            ]
 
     def take(c, stage):
-        flying[c].wait_recv()
-        bit, dim = orders[c % 2][stage]
-        news = list(index[c])
-        news[dim] = 1 - bit_value(bit)
-        index[c][dim] = slice(None)
+        bits, dims = orders[c % 2][stage]
+        fresh = []
+        for move, copy in reversed(flying[c]):
+            copy.wait_recv()
+            news = list(index[c])
+            for i, dim in enumerate(dims):
+                news[dim] = flipped(bits[i], i, move)
+            fresh.append((move, news))
+        for dim in dims:
+            index[c][dim] = slice(None)
         give(c, stage + 1)
-        late.append(push(news, c, core_bit, send_core.at[c, stage], recv_core.at[c, stage]))
-
-    ahead, behind = (0, 1), (2, 3)
-    for c in ahead:
+        for move, news in fresh:
+            late.append(
+                push(
+                    news,
+                    c,
+                    core_bits,
+                    1,
+                    send_core.at[c, stage, move - 1],
+                    recv_core.at[c, stage, move - 1],
+                )
+            )
+
+    turn = (2, 3, 0, 1)
+    for c in turn:
         give(c, 0)
-    for stage in range(HEAD_BITS + 2):
-        for c in ahead:
-            if stage < HEAD_BITS:
-                take(c, stage)
-        for c in behind:
-            if stage == 1:
-                give(c, 0)
-            if stage >= 2:
-                take(c, stage - 2)
+    for stage in range(stage_count):
+        for c in turn:
+            take(c, stage)
     for copy in late:
         copy.wait_recv()
     for copy in sent:
@@ -461,23 +500,28 @@
     )(heads, features, ids, goals, station_weight)
 
     core_bit, owner, rest = bits_of(mesh_shape)
-    named = [(bit, dim) for dim, bit in enumerate(owner)]
-    x, y, z0, z1 = named
-    tail = [(bit, None) for bit in rest]
-    down = ([x, y, z0, z1] + tail, [y, x, z0, z1] + tail)
-    up = ([z1, z0, y, x], [z1, z0, x, y])
+    core = (core_bit,)
+    x, y = ((owner[0],), (0,)), ((owner[1],), (1,))
+    z = ((owner[2], owner[3]), (2, 3))
+    tail = [((bit,), ()) for bit in rest]
+    down = ([x, y, z] + tail, [y, x, z] + tail)
+    up = ([z, y, x], [z, x, y])
+    groups_up = [core] + [bits for bits, _ in up[0]]
+    groups_down = groups_up + [bits for bits, _ in tail]
+    partners = 3
     dims = (2,) * HEAD_BITS
     half = PACK_ROWS // 2
     count = len(CHAINS)
     buffers = []
     for c, (_, size) in enumerate(CHAINS):
         free = HEAD_BITS
-        for bit, dim in down[c % 2]:
-            free -= dim is not None
-            buffers.append(pltpu.VMEM((2,) * free + (size, LANES), F32))
+        for bits, spots in down[c % 2]:
+            free -= len(spots)
+            shape = (len(moves_of(bits)),) + (2,) * free + (size, LANES)
+            buffers.append(pltpu.VMEM(shape, F32))
     vmem = pl.BlockSpec(memory_space=pltpu.VMEM)
     summed = pl.pallas_call(
-        functools.partial(reduce_kernel, (core_bit, down, [core_bit] + owner + rest)),
+        functools.partial(reduce_kernel, (core, down, groups_down)),
         out_shape=jax.ShapeDtypeStruct((PACK_ROWS, LANES), F32),
         in_specs=[vmem],
         out_specs=vmem,
@@ -486,8 +530,8 @@
             pltpu.VMEM((*dims, half, LANES), F32),
             pltpu.VMEM((half, LANES), F32),
             *buffers,
-            pltpu.SemaphoreType.DMA((count, len(down[0]) + 2)),
-            pltpu.SemaphoreType.DMA((count, len(down[0]) + 2)),
+            pltpu.SemaphoreType.DMA((count, len(down[0]) + 2, partners)),
+            pltpu.SemaphoreType.DMA((count, len(down[0]) + 2, partners)),
         ],
         compiler_params=pltpu.CompilerParams(
             collective_id=0, has_side_effects=True, vmem_limit_bytes=big
@@ -505,15 +549,15 @@
     )(summed)
 
     everyone = pl.pallas_call(
-        functools.partial(gather_kernel, (core_bit, up, [core_bit] + owner)),
+        functools.partial(gather_kernel, (core, up, groups_up)),
         out_shape=jax.ShapeDtypeStruct((*dims, PACK_ROWS, LANES), F32),
         in_specs=[vmem],
         out_specs=vmem,
         scratch_shapes=[
-            pltpu.SemaphoreType.DMA((count, HEAD_BITS)),
-            pltpu.SemaphoreType.DMA((count, HEAD_BITS)),
-            pltpu.SemaphoreType.DMA((count, HEAD_BITS)),
-            pltpu.SemaphoreType.DMA((count, HEAD_BITS)),
+            pltpu.SemaphoreType.DMA((count, len(up[0]), partners)),
+            pltpu.SemaphoreType.DMA((count, len(up[0]), partners)),
+            pltpu.SemaphoreType.DMA((count, len(up[0]), partners)),
+            pltpu.SemaphoreType.DMA((count, len(up[0]), partners)),
         ],
         compiler_params=pltpu.CompilerParams(
             collective_id=1, has_side_effects=True, vmem_limit_bytes=big

time: 91.6 us -> 85.8 us (0.937)
  Pallas kernels: 87 us -> 81.6 us
    pallas_call x2, Pallas kernels: 58.7 us -> 54.3 us  [the longest x1 29.1 us: local(): pl.pallas_call(functools.partial(reduce_kernel, (core, down, groups_down)...]
    pallas_call x1, Pallas kernels: 11.4 us -> 10.4 us  [local(): pl.pallas_call(gram_kernel, grid=(blocks // per,), in_specs=[away, feat_s...]
where the time goes in v3:
time: 85.8 us; the launch traced here: 85.4 us
  Pallas kernels  81.6 us (95%)
  local copies, waits for them, and re-layouts  3.09 us (4%)
    pallas_call x1, Pallas kernels, local(): pl.pallas_call(functools.partial(reduce_kernel, (core, down, groups_down)...  29.1 us
    pallas_call x1, Pallas kernels, local(): pl.pallas_call(functools.partial(gather_kernel, (core, up, groups_up)), o...  25.2 us
    pallas_call x1, Pallas kernels, local(): pl.pallas_call(gram_kernel, grid=(blocks // per,), in_specs=[away, feat_s...  10.4 us
    pallas_call x1, Pallas kernels, local(): pl.pallas_call(factor_kernel, out_shape=jax.ShapeDtypeStruct((PACK_ROWS,...  10.1 us
    pallas_call x1, Pallas kernels, local(): pl.pallas_call(functools.partial(leverage_kernel, scale), grid=(blocks //...  6.8 us
    unnamed x10, local copies, waits for them, and re-layouts  3.09 us

profile of v3, /device:TPU:0, one launch (start us, length us, event | category | flops | bytes accessed | tf_op | source)
XLA Modules:
  0.0 85.4 jit_solution(12785144813767967222)
XLA Ops:
  0.6 0.0 copy-start
  0.6 0.8 copy-done
  1.5 0.0 copy-start.2
  1.5 0.8 copy-done.2
  2.3 0.0 copy-start.3
  2.3 0.8 copy-done.3
  3.1 0.0 copy-start.4
  3.1 0.7 copy-done.4
  3.7 10.4 %gram.1 = (f32[16,336,128]{2,1,0:T(8,128)S(1)}, f32[128,128]{1,0:T(8,128)S(1)}) custom-call(s32[128,128]{1,0:T(8,128)S(1)} %bitcast.9, bf16[16384,256]{1,0:T(8,128)(2,1)} %feat_ref.3, s32[128,128]{1,0:T(8,128)S(1)} %bitcast.11, bf16[128,128]{1,0:T(8,128)(2,1)S(1)} %bitcast.12, f32[1,128]{1,0:T(1,128)S(1)} %copy-done.4), custom_call_target="tpu_custom_call" | custom-call | tf_op jit(solution)/shard_map/gram/pallas_call | solution.py:473
  14.1 0.0 copy-start.1
  14.1 29.1 %reduce.1.g_ref = f32[336,128]{1,0:T(8,128)S(1)} custom-call(f32[2,2,2,2,336,128]{5,4,3,2,1,0:T(8,128)S(1)} %bitcast.8), custom_call_target="tpu_custom_call" | custom-call | tf_op jit(solution)/shard_map/reduce/pallas_call | solution.py:523
  43.2 10.1 %factor.1.x_ref = f32[336,128]{1,0:T(8,128)S(1)} custom-call(f32[336,128]{1,0:T(8,128)S(1)} %reduce.1.g_ref), custom_call_target="tpu_custom_call" | custom-call | tf_op jit(solution)/shard_map/factor/pallas_call | solution.py:542
  53.3 25.2 %gather.1 = f32[2,2,2,2,336,128]{5,4,3,2,1,0:T(8,128)S(1)} custom-call(f32[336,128]{1,0:T(8,128)S(1)} %factor.1.x_ref), custom_call_target="tpu_custom_call" | custom-call | tf_op jit(solution)/shard_map/gather/pallas_call | solution.py:551
  78.6 0.0 copy-done.1
  78.6 6.8 %leverage.1 = (f32[128,128]{1,0:T(8,128)}, f32[16,256]{1,0:T(8,128)}, f32[16,16,256]{2,1,0:T(8,128)}) custom-call(s32[1]{0:T(128)} %bitcast.place_ref, s32[128,128]{1,0:T(8,128)S(1)} %bitcast.10, bf16[16384,256]{1,0:T(8,128)(2,1)} %feat_ref.3, f32[128,128]{1,0:T(8,128)S(1)} %get-tuple-element.8.w_ref, f32[16,336,128]{2,1,0:T(8,128)S(1)} %bitcast.7), custom_call_target="tpu_custom_call" | custom-call | tf_op jit(solution)/shard_map/leverage/pallas_call | solution.py:570
Async XLA Ops:
  0.6 0.8 copy-start
  1.5 0.8 copy-start.2
  2.3 0.8 copy-start.3
  3.1 0.7 copy-start.4
  14.1 64.4 %copy-start.1 = (s32[16384]{0:T(1024)S(1)}, s32[16384]{0:T(1024)}, u32[]{:S(2)}) copy-start(s32[16384]{0:T(1024)} %param.8) | copy-start | bytes 196612

commit v4 on v3

--- a/solution.py
+++ b/solution.py
@@ -69,34 +69,25 @@
 
 
 def gram_kernel(
-    heads_hbm, feat_ref, ids_hbm, tgt_hbm, table_hbm, out_ref, w_ref, acc, vec, heads, ids, low, tgt, table, sems
+    feat_ref, code_ref, tgt_ref, table_ref, out_ref, w_ref, acc, vec, codes, sem
 ):
     step = pl.program_id(0)
     per = feat_ref.shape[0] // BLK
 
     @pl.when(step == 0)
     def _():
-        copies = [
-            pltpu.make_async_copy(src, dst, sems.at[i])
-            for i, (src, dst) in enumerate(
-                ((ids_hbm, ids), (table_hbm, table), (tgt_hbm, low), (heads_hbm, heads))
-            )
-        ]
-        for copy in copies:
-            copy.start()
+        copy = pltpu.make_async_copy(code_ref, codes, sem)
+        copy.start()
         acc[...] = jnp.zeros_like(acc)
         vec[...] = jnp.zeros_like(vec)
-        for copy in copies:
-            copy.wait()
-        tgt[...] = low[...].astype(F32)
-
-    lookup = jnp.broadcast_to(table[...], (SUB, LANES))
+        copy.wait()
+
+    lookup = jnp.broadcast_to(table_ref[...], (SUB, LANES))
     row = lax.broadcasted_iota(jnp.int32, (SUB, LANES), 0)
     for i in range(per):
         line = pl.multiple_of((step * per + i) * SUB, SUB)
-        weights = jnp.take_along_axis(
-            lookup, ids[pl.ds(line, SUB), :], axis=1, mode="promise_in_bounds"
-        )
+        ids = jnp.bitwise_and(code_ref[pl.ds(line, SUB), :], LANES - 1)
+        weights = jnp.take_along_axis(lookup, ids, axis=1, mode="promise_in_bounds")
         w_ref[i * SUB : (i + 1) * SUB, :] = weights
         feat = feat_ref[i * BLK : (i + 1) * BLK, :]
         turned = feat.T
@@ -109,9 +100,9 @@
             ],
             axis=1,
         )
-        head = heads[line, 0]
+        head = lax.div(codes[line, 0], LANES)
         acc[head] += jnp.dot(scaled, feat, preferred_element_type=F32)
-        here = tgt[pl.ds(line, SUB), :]
+        here = tgt_ref[pl.ds(line, SUB), :]
         spread = jnp.concatenate([jnp.where(row == c, here, 0.0) for c in range(SUB)], axis=1)
         vec[head] += lax.dot_general(
             spread.astype(jnp.bfloat16),
@@ -315,7 +306,12 @@
             cols = [jnp.broadcast_to(rows[g][:, j : j + 1], (8, LANES)) for j in columns]
             for k in range(8):
                 if g == p:
-                    pivots[k] = 1.0 / cols[k][k : k + 1, :]
+                    if k % 2 == 0:
+                        a = cols[k][k : k + 1, :]
+                        b = cols[k + 1][k : k + 1, :]
+                        d = cols[k + 1][k + 1 : k + 2, :]
+                        pivots[k] = 1.0 / a
+                        pivots[k + 1] = a * (1.0 / (a * d - b * b))
                     lines[k] = rows[p][k : k + 1, :]
                     for m in range(k + 1, 8):
                         across[k][m] = cols[m][k : k + 1, :]
@@ -461,24 +457,22 @@
     tm = mesh_shape["tm"]
     total_rows = row_count * mesh_shape["station"] * tm
     scale = total_rows / (HEADS * width)
-    ids = station_ids.reshape(lines, LANES)
     heads = lead_heads.reshape(lines, LANES)
-    goals = targets.reshape(lines, LANES)
+    codes = (lead_heads * LANES + station_ids).reshape(lines, LANES)
+    goals = targets.astype(F32).reshape(lines, LANES)
     per = math.gcd(blocks, 4)
     head_spec = pl.BlockSpec((per * SUB, LANES), lambda b: (b, 0), memory_space=pltpu.SMEM)
     line_spec = pl.BlockSpec((per * SUB, LANES), lambda b: (b, 0))
     feat_spec = pl.BlockSpec((per * BLK, width), lambda b: (b, 0))
-    away = pl.BlockSpec(memory_space=pltpu.HBM)
     big = 48 * 1024 * 1024
     packed, weights = pl.pallas_call(
         gram_kernel,
         grid=(blocks // per,),
         in_specs=[
-            away,
             feat_spec,
-            away,
-            away,
-            away,
+            pl.BlockSpec((lines, LANES), lambda b: (0, 0)),
+            pl.BlockSpec((lines, LANES), lambda b: (0, 0)),
+            pl.BlockSpec((1, LANES), lambda b: (0, 0)),
         ],
         out_specs=[pl.BlockSpec((HEADS, PACK_ROWS, LANES), lambda b: (0, 0, 0)), line_spec],
         out_shape=[
@@ -489,15 +483,11 @@
             pltpu.VMEM((HEADS, width, width), F32),
             pltpu.VMEM((HEADS, 8, width), F32),
             pltpu.SMEM((lines, LANES), jnp.int32),
-            pltpu.VMEM((lines, LANES), jnp.int32),
-            pltpu.VMEM((lines, LANES), jnp.bfloat16),
-            pltpu.VMEM((lines, LANES), F32),
-            pltpu.VMEM(station_weight.shape, F32),
-            pltpu.SemaphoreType.DMA((4,)),
+            pltpu.SemaphoreType.DMA,
         ],
         compiler_params=pltpu.CompilerParams(vmem_limit_bytes=big),
         name="gram",
-    )(heads, features, ids, goals, station_weight)
+    )(features, codes, goals, station_weight)
 
     core_bit, owner, rest = bits_of(mesh_shape)
     core = (core_bit,)

time: 85.8 us -> 84.1 us (0.980)
  local copies, waits for them, and re-layouts: 3.09 us -> 0.66 us
  other arithmetic: 0 us -> 1.64 us
  Pallas kernels: 81.6 us -> 80.7 us
    unnamed x10 -> x4, local copies, waits for them, and re-layouts: 3.09 us -> 0.66 us
    reshape x0 -> x2, other arithmetic: none -> 1.64 us  [the longest x1 0.88 us: local(): codes = (lead_heads * LANES + station_ids).reshape(lines, LANES)]
where the time goes in v4:
time: 84.1 us; the launch traced here: 83.7 us
  Pallas kernels  80.7 us (96%)
  other arithmetic  1.64 us (2%)
    pallas_call x1, Pallas kernels, local(): pl.pallas_call(functools.partial(reduce_kernel, (core, down, groups_down)...  29.1 us
    pallas_call x1, Pallas kernels, local(): pl.pallas_call(functools.partial(gather_kernel, (core, up, groups_up)), o...  25.2 us
    pallas_call x1, Pallas kernels, local(): pl.pallas_call(gram_kernel, grid=(blocks // per,), in_specs=[feat_spec, p...  10.3 us
    pallas_call x1, Pallas kernels, local(): pl.pallas_call(factor_kernel, out_shape=jax.ShapeDtypeStruct((PACK_ROWS,...  9.37 us
    pallas_call x1, Pallas kernels, local(): pl.pallas_call(functools.partial(leverage_kernel, scale), grid=(blocks //...  6.8 us

profile of v4, /device:TPU:0, one launch (start us, length us, event | category | flops | bytes accessed | tf_op | source)
XLA Modules:
  0.0 83.7 jit_solution(12324633616167388487)
XLA Ops:
  0.6 0.8 bitcast_convert_fusion.tgt_ref
  1.4 0.9 %add_bitcast_fusion.code_ref = s32[128,128]{1,0:T(8,128)S(1)} fusion(s32[16384]{0:T(1024)} %param.7, s32[16384]{0:T(1024)} %param.8), kind=kLoop, calls=%fused_computation | loop fusion | flops 32768 | bytes 196608 | tf_op jit(solution)/shard_map/reshape | solution.py:461
  2.3 0.0 copy-start.1
  2.3 0.6 copy-done.1
  2.9 10.3 %gram.1 = (f32[16,336,128]{2,1,0:T(8,128)S(1)}, f32[128,128]{1,0:T(8,128)S(1)}) custom-call(bf16[16384,256]{1,0:T(8,128)(2,1)} %feat_ref.3, s32[128,128]{1,0:T(8,128)S(1)} %add_bitcast_fusion.code_ref, f32[128,128]{1,0:T(8,128)S(1)} %bitcast_convert_fusion.tgt_ref, f32[1,128]{1,0:T(1,128)S(1)} %copy-done.1), custom_call_target="tpu_custom_call" | custom-call | tf_op jit(solution)/shard_map/gram/pallas_call | solution.py:468
  13.2 0.0 copy-start
  13.2 29.1 %reduce.1.g_ref = f32[336,128]{1,0:T(8,128)S(1)} custom-call(f32[2,2,2,2,336,128]{5,4,3,2,1,0:T(8,128)S(1)} %bitcast.11), custom_call_target="tpu_custom_call" | custom-call | tf_op jit(solution)/shard_map/reduce/pallas_call | solution.py:513
  42.3 9.4 %factor.1.x_ref = f32[336,128]{1,0:T(8,128)S(1)} custom-call(f32[336,128]{1,0:T(8,128)S(1)} %reduce.1.g_ref), custom_call_target="tpu_custom_call" | custom-call | tf_op jit(solution)/shard_map/factor/pallas_call | solution.py:532
  51.7 25.2 %gather.1 = f32[2,2,2,2,336,128]{5,4,3,2,1,0:T(8,128)S(1)} custom-call(f32[336,128]{1,0:T(8,128)S(1)} %factor.1.x_ref), custom_call_target="tpu_custom_call" | custom-call | tf_op jit(solution)/shard_map/gather/pallas_call | solution.py:541
  76.9 0.0 copy-done
  76.9 6.8 %leverage.1 = (f32[128,128]{1,0:T(8,128)}, f32[16,256]{1,0:T(8,128)}, f32[16,16,256]{2,1,0:T(8,128)}) custom-call(s32[1]{0:T(128)} %bitcast.place_ref, s32[128,128]{1,0:T(8,128)S(1)} %bitcast.12, bf16[16384,256]{1,0:T(8,128)(2,1)} %feat_ref.3, f32[128,128]{1,0:T(8,128)S(1)} %get-tuple-element.8.w_ref, f32[16,336,128]{2,1,0:T(8,128)S(1)} %bitcast.10), custom_call_target="tpu_custom_call" | custom-call | tf_op jit(solution)/shard_map/leverage/pallas_call | solution.py:560
Async XLA Ops:
  2.3 0.7 copy-start.1
  13.2 63.7 %copy-start = (s32[16384]{0:T(1024)S(1)}, s32[16384]{0:T(1024)}, u32[]{:S(2)}) copy-start(s32[16384]{0:T(1024)} %param.8) | copy-start | bytes 196612

commit v5 on v4

--- a/solution.py
+++ b/solution.py
@@ -52,7 +52,7 @@
     return 1 - value if (move >> i) & 1 else value
 
 
-def greet(groups):
+def call_out(groups):
     barrier = pltpu.get_barrier_semaphore()
     met = 0
     for bits in groups:
@@ -61,7 +61,11 @@
                 barrier, inc=1, device_id=partner(bits, move), device_id_type=MESH
             )
             met += 1
-    pl.semaphore_wait(barrier, met)
+    return met
+
+
+def hear(met):
+    pl.semaphore_wait(pltpu.get_barrier_semaphore(), met)
 
 
 def half_tiles(full):
@@ -141,7 +145,7 @@
     own = [pl.ds(start, size) for start, size in CHAINS]
     mine = [pl.ds(pl.multiple_of(core * half + start, 8), size) for start, size in CHAINS]
     theirs = [pl.ds(pl.multiple_of((1 - core) * half + start, 8), size) for start, size in CHAINS]
-    greet(groups)
+    hear(call_out(groups))
     sent = []
     flying = [[] for _ in range(count)]
     index = [[slice(None)] * HEAD_BITS for _ in range(count)]
@@ -203,7 +207,7 @@
         copy.wait_send()
 
 
-def gather_kernel(plan, x_ref, out_ref, send, recv, send_core, recv_core):
+def gather_kernel(plan, g_ref, out_ref, send, recv, send_core, recv_core):
     core_bits, orders, groups = plan
     count = len(CHAINS)
     half = PACK_ROWS // 2
@@ -213,8 +217,9 @@
     for bits, dims in orders[0]:
         for bit, dim in zip(bits, dims):
             own[dim] = bit_value(bit)
-    out_ref[(*own,)] = x_ref[...]
-    greet(groups)
+    met = call_out(groups)
+    solve_head(g_ref, out_ref.at[(*own,)])
+    hear(met)
     sent, late = [], []
 
     def push(place, chain, bits, move, send_sem, recv_sem):
@@ -346,7 +351,7 @@
     return x1, x21 + x2
 
 
-def factor_kernel(g_ref, out_ref):
+def solve_head(g_ref, out_ref):
     lane = lax.broadcasted_iota(jnp.int32, (64, LANES), 1)
     row = lax.broadcasted_iota(jnp.int32, (64, LANES), 0)
     low = lane < 64
@@ -529,15 +534,6 @@
         name="reduce",
     )(packed.reshape(*dims, PACK_ROWS, LANES))
 
-    solved = pl.pallas_call(
-        factor_kernel,
-        out_shape=jax.ShapeDtypeStruct((PACK_ROWS, LANES), F32),
-        in_specs=[vmem],
-        out_specs=vmem,
-        compiler_params=pltpu.CompilerParams(vmem_limit_bytes=big),
-        name="factor",
-    )(summed)
-
     everyone = pl.pallas_call(
         functools.partial(gather_kernel, (core, up, groups_up)),
         out_shape=jax.ShapeDtypeStruct((*dims, PACK_ROWS, LANES), F32),
@@ -553,7 +549,7 @@
             collective_id=1, has_side_effects=True, vmem_limit_bytes=big
         ),
         name="gather",
-    )(solved).reshape(HEADS, PACK_ROWS, LANES)
+    )(summed).reshape(HEADS, PACK_ROWS, LANES)
 
     piece_rows = width // tm
     place = lax.axis_index("tm").reshape(1).astype(jnp.int32)

time: 84.1 us -> 82.5 us (0.981)
  Pallas kernels: 80.7 us -> 79.2 us
    pallas_call x1 -> x0, Pallas kernels: 9.37 us -> none  [local(): pl.pallas_call(factor_kernel, out_shape=jax.ShapeDtypeStruct((PACK_ROWS,...]
    pallas_call x1, Pallas kernels: 25.2 us -> 33 us  [local(): pl.pallas_call(functools.partial(gather_kernel, (core, up, groups_up)), o...]
where the time goes in v5:
time: 82.5 us; the launch traced here: 82.1 us
  Pallas kernels  79.2 us (96%)
  other arithmetic  1.64 us (2%)
    pallas_call x1, Pallas kernels, local(): pl.pallas_call(functools.partial(gather_kernel, (core, up, groups_up)), o...  33 us
    pallas_call x1, Pallas kernels, local(): pl.pallas_call(functools.partial(reduce_kernel, (core, down, groups_down)...  29.1 us
    pallas_call x1, Pallas kernels, local(): pl.pallas_call(gram_kernel, grid=(blocks // per,), in_specs=[feat_spec, p...  10.3 us
    pallas_call x1, Pallas kernels, local(): pl.pallas_call(functools.partial(leverage_kernel, scale), grid=(blocks //...  6.8 us

profile of v5, /device:TPU:0, one launch (start us, length us, event | category | flops | bytes accessed | tf_op | source)
XLA Modules:
  0.0 82.1 jit_solution(16322994990549438241)
XLA Ops:
  0.6 0.8 bitcast_convert_fusion.tgt_ref
  1.4 0.9 %add_bitcast_fusion.code_ref = s32[128,128]{1,0:T(8,128)S(1)} fusion(s32[16384]{0:T(1024)} %param.7, s32[16384]{0:T(1024)} %param.8), kind=kLoop, calls=%fused_computation | loop fusion | flops 32768 | bytes 196608 | tf_op jit(solution)/shard_map/reshape | solution.py:466
  2.3 0.0 copy-start.1
  2.3 0.6 copy-done.1
  2.9 10.3 %gram.1 = (f32[16,336,128]{2,1,0:T(8,128)S(1)}, f32[128,128]{1,0:T(8,128)S(1)}) custom-call(bf16[16384,256]{1,0:T(8,128)(2,1)} %feat_ref.3, s32[128,128]{1,0:T(8,128)S(1)} %add_bitcast_fusion.code_ref, f32[128,128]{1,0:T(8,128)S(1)} %bitcast_convert_fusion.tgt_ref, f32[1,128]{1,0:T(1,128)S(1)} %copy-done.1), custom_call_target="tpu_custom_call" | custom-call | tf_op jit(solution)/shard_map/gram/pallas_call | solution.py:473
  13.2 0.0 copy-start
  13.2 29.1 %reduce.1.g_ref = f32[336,128]{1,0:T(8,128)S(1)} custom-call(f32[2,2,2,2,336,128]{5,4,3,2,1,0:T(8,128)S(1)} %bitcast.11), custom_call_target="tpu_custom_call" | custom-call | tf_op jit(solution)/shard_map/reduce/pallas_call | solution.py:518
  42.3 33.0 %gather.1 = f32[2,2,2,2,336,128]{5,4,3,2,1,0:T(8,128)S(1)} custom-call(f32[336,128]{1,0:T(8,128)S(1)} %reduce.1.g_ref), custom_call_target="tpu_custom_call" | custom-call | tf_op jit(solution)/shard_map/gather/pallas_call | solution.py:537
  75.3 0.0 copy-done
  75.3 6.8 %leverage.1 = (f32[128,128]{1,0:T(8,128)}, f32[16,256]{1,0:T(8,128)}, f32[16,16,256]{2,1,0:T(8,128)}) custom-call(s32[1]{0:T(128)} %bitcast.place_ref, s32[128,128]{1,0:T(8,128)S(1)} %bitcast.12, bf16[16384,256]{1,0:T(8,128)(2,1)} %feat_ref.3, f32[128,128]{1,0:T(8,128)S(1)} %get-tuple-element.8.w_ref, f32[16,336,128]{2,1,0:T(8,128)S(1)} %bitcast.10), custom_call_target="tpu_custom_call" | custom-call | tf_op jit(solution)/shard_map/leverage/pallas_call | solution.py:556
Async XLA Ops:
  2.3 0.7 copy-start.1
  13.2 62.1 %copy-start = (s32[16384]{0:T(1024)S(1)}, s32[16384]{0:T(1024)}, u32[]{:S(2)}) copy-start(s32[16384]{0:T(1024)} %param.8) | copy-start | bytes 196612

commit v6 on v5

--- a/solution.py
+++ b/solution.py
@@ -470,6 +470,7 @@
     line_spec = pl.BlockSpec((per * SUB, LANES), lambda b: (b, 0))
     feat_spec = pl.BlockSpec((per * BLK, width), lambda b: (b, 0))
     big = 48 * 1024 * 1024
+    small = 20 * 1024 * 1024
     packed, weights = pl.pallas_call(
         gram_kernel,
         grid=(blocks // per,),
@@ -529,7 +530,7 @@
             pltpu.SemaphoreType.DMA((count, len(down[0]) + 2, partners)),
         ],
         compiler_params=pltpu.CompilerParams(
-            collective_id=0, has_side_effects=True, vmem_limit_bytes=big
+            collective_id=0, has_side_effects=True, vmem_limit_bytes=small
         ),
         name="reduce",
     )(packed.reshape(*dims, PACK_ROWS, LANES))
@@ -546,7 +547,7 @@
             pltpu.SemaphoreType.DMA((count, len(up[0]), partners)),
         ],
         compiler_params=pltpu.CompilerParams(
-            collective_id=1, has_side_effects=True, vmem_limit_bytes=big
+            collective_id=1, has_side_effects=True, vmem_limit_bytes=small
         ),
         name="gather",
     )(summed).reshape(HEADS, PACK_ROWS, LANES)
@@ -573,7 +574,7 @@
             jax.ShapeDtypeStruct((HEADS, width), F32),
             jax.ShapeDtypeStruct((HEADS, piece_rows, width), F32),
         ],
-        compiler_params=pltpu.CompilerParams(vmem_limit_bytes=big),
+        compiler_params=pltpu.CompilerParams(vmem_limit_bytes=small),
         name="leverage",
     )(place, heads, features, weights, everyone)
     return (leverage.reshape(row_count), zscores, pieces)

time: 82.5 us -> 81 us (0.982)
  Pallas kernels: 79.2 us -> 77.7 us
    pallas_call x1, Pallas kernels: 6.8 us -> 5.19 us  [local(): pl.pallas_call(functools.partial(leverage_kernel, scale), grid=(blocks //...]
where the time goes in v6:
time: 81 us; the launch traced here: 80.7 us
  Pallas kernels  77.7 us (96%)
  other arithmetic  1.64 us (2%)
    pallas_call x1, Pallas kernels, local(): pl.pallas_call(functools.partial(gather_kernel, (core, up, groups_up)), o...  33 us
    pallas_call x1, Pallas kernels, local(): pl.pallas_call(functools.partial(reduce_kernel, (core, down, groups_down)...  29.1 us
    pallas_call x1, Pallas kernels, local(): pl.pallas_call(gram_kernel, grid=(blocks // per,), in_specs=[feat_spec, p...  10.4 us
    pallas_call x1, Pallas kernels, local(): pl.pallas_call(functools.partial(leverage_kernel, scale), grid=(blocks //...  5.19 us

profile of v6, /device:TPU:0, one launch (start us, length us, event | category | flops | bytes accessed | tf_op | source)
XLA Modules:
  0.0 80.7 jit_solution(12248264425544236783)
XLA Ops:
  0.6 0.8 bitcast_convert_fusion.tgt_ref
  1.4 0.9 %add_bitcast_fusion.code_ref = s32[128,128]{1,0:T(8,128)S(1)} fusion(s32[16384]{0:T(1024)} %param.7, s32[16384]{0:T(1024)} %param.8), kind=kLoop, calls=%fused_computation | loop fusion | flops 32768 | bytes 196608 | tf_op jit(solution)/shard_map/reshape | solution.py:466
  2.3 0.0 copy-start.2
  2.3 0.6 copy-done.2
  2.9 0.0 copy-start
  2.9 10.4 %gram.1 = (f32[16,336,128]{2,1,0:T(8,128)S(1)}, f32[128,128]{1,0:T(8,128)S(1)}) custom-call(bf16[16384,256]{1,0:T(8,128)(2,1)} %feat_ref.3, s32[128,128]{1,0:T(8,128)S(1)} %add_bitcast_fusion.code_ref, f32[128,128]{1,0:T(8,128)S(1)} %bitcast_convert_fusion.tgt_ref, f32[1,128]{1,0:T(1,128)S(1)} %copy-done.2), custom_call_target="tpu_custom_call" | custom-call | tf_op jit(solution)/shard_map/gram/pallas_call | solution.py:474
  13.4 0.0 copy-start.1
  13.4 29.1 %reduce.1.g_ref = f32[336,128]{1,0:T(8,128)S(1)} custom-call(f32[2,2,2,2,336,128]{5,4,3,2,1,0:T(8,128)S(1)} %bitcast.11), custom_call_target="tpu_custom_call" | custom-call | tf_op jit(solution)/shard_map/reduce/pallas_call | solution.py:519
  42.5 33.0 %gather.1 = f32[2,2,2,2,336,128]{5,4,3,2,1,0:T(8,128)S(1)} custom-call(f32[336,128]{1,0:T(8,128)S(1)} %reduce.1.g_ref), custom_call_target="tpu_custom_call" | custom-call | tf_op jit(solution)/shard_map/gather/pallas_call | solution.py:538
  75.5 0.0 copy-done
  75.5 0.0 copy-done.1
  75.5 5.2 %leverage.1 = (f32[128,128]{1,0:T(8,128)}, f32[16,256]{1,0:T(8,128)}, f32[16,16,256]{2,1,0:T(8,128)}) custom-call(s32[1]{0:T(128)} %bitcast.place_ref, s32[128,128]{1,0:T(8,128)S(1)} %bitcast.12, bf16[16384,256]{1,0:T(8,128)(2,1)S(1)} %copy-done, f32[128,128]{1,0:T(8,128)S(1)} %get-tuple-element.8.w_ref, f32[16,336,128]{2,1,0:T(8,128)S(1)} %bitcast.10), custom_call_target="tpu_custom_call" | custom-call | tf_op jit(solution)/shard_map/leverage/pallas_call | solution.py:557
Async XLA Ops:
  2.3 0.7 copy-start.2
  2.9 72.5 %copy-start = (bf16[16384,256]{1,0:T(8,128)(2,1)S(1)}, bf16[16384,256]{1,0:T(8,128)(2,1)}, u32[]{:S(2)}) copy-start(bf16[16384,256]{1,0:T(8,128)(2,1)} %feat_ref.3) | copy-start | bytes 25165828
  13.4 62.1 %copy-start.1 = (s32[16384]{0:T(1024)S(1)}, s32[16384]{0:T(1024)}, u32[]{:S(2)}) copy-start(s32[16384]{0:T(1024)} %param.8) | copy-start | bytes 196612
